TPU v7x, 32 devices: a whole 2x2x4 slice. The times are simulated.
32 devices in a mesh: ctx: 8 (over z, core), head: 4 (over y, x).
Axes of the slice: x: 2, y: 2, z: 4, core: 2. Of those that a mesh axis runs over, the one named last changes fastest.
Arguments:
- queries: bfloat16 [2048, 32, 128], P('ctx', 'head'), may hold values from -8 to 8
- key_proj: bfloat16 [2048, 4, 128], P(('ctx', 'head')), may hold values from -8 to 8
- value_proj: bfloat16 [2048, 4, 128], P(('ctx', 'head')), may hold values from -6 to 6
- out_grad: bfloat16 [2048, 32, 128], P('ctx', 'head'), may hold values from -6 to 6
- tile_order: int32 [16], replicated, may hold values from 0 to 15, each once
- doc_tiles: int32 [4], replicated, may hold values from 1 to 8, 16 in all
Outputs:
- attended: bfloat16 [2048, 32, 128], P('ctx', 'head')
- query_grad: bfloat16 [2048, 32, 128], P('ctx', 'head')
- key_grad: bfloat16 [2048, 4, 128], P(('ctx', 'head'))
- value_grad: bfloat16 [2048, 4, 128], P(('ctx', 'head'))
Inputs may be any that keep to these rules, and one draw needn't show every extreme that they name: `tile_order`: a permutation of the 16 tiles. `doc_tiles`: positive lengths in tiles summing to 16.
All inputs are finite; a program needn't handle non-finite values.
Results may differ from a plain program's by a relative error of at most 0.02.
Values may be sent and summed in bfloat16 or wider, within the bound.
A program may use at most 64 MiB of HBM per device.

v0:
```python
import math
import jax
import jax.numpy as jnp
from jax import lax
from jax.sharding import PartitionSpec as P

TILE = 128
NEG = -1e30


def from_behind(value, axis, steps):
    count = lax.axis_size(axis)
    pairs = [(source, (source + steps) % count) for source in range(count)]
    return lax.ppermute(value, axis, pairs)


def row_info(tile_order, doc_ends, shard, row_count, tile_len):
    per_shard = row_count // tile_len
    shard_tiles = lax.dynamic_slice_in_dim(tile_order, shard * per_shard, per_shard)
    tile_doc = jnp.sum((shard_tiles[:, None] >= doc_ends[None, :]).astype(jnp.int32), axis=1)
    offsets = jnp.arange(tile_len, dtype=jnp.int32)
    positions = (shard_tiles[:, None] * tile_len + offsets[None, :]).reshape(-1)
    documents = jnp.broadcast_to(tile_doc[:, None], (per_shard, tile_len)).reshape(-1)
    return (positions, documents, shard_tiles, tile_doc)


def block_scores(query_block, key_block, score_scale):
    return (
        jnp.einsum("tngd,knd->tngk", query_block, key_block, preferred_element_type=jnp.float32)
        * score_scale
    )


def forward_block(carried, query_block, key_block, value_block, allowed, score_scale):
    running_max, running_sum, accumulated = carried
    scores = block_scores(query_block, key_block, score_scale)
    visible = allowed[:, None, None, :]
    block_max = jnp.max(jnp.where(visible, scores, NEG), axis=-1)
    new_max = jnp.maximum(running_max, block_max)
    weights = jnp.where(visible, jnp.exp(scores - new_max[..., None]), 0.0)
    factor = jnp.exp(running_max - new_max)
    running_sum = running_sum * factor + jnp.sum(weights, axis=-1)
    product = jnp.einsum(
        "tngk,knd->tngd",
        weights.astype(jnp.bfloat16),
        value_block,
        preferred_element_type=jnp.float32,
    )
    accumulated = accumulated * factor[..., None] + product
    return (new_max, running_sum, accumulated)


def backward_block(
    query_block, grad_block, log_sum, delta, key_block, value_block, allowed, score_scale
):
    scores = block_scores(query_block, key_block, score_scale)
    visible = allowed[:, None, None, :]
    probs = jnp.where(visible, jnp.exp(scores - log_sum[..., None]), 0.0)
    value_add = jnp.einsum(
        "tngk,tngd->knd", probs.astype(jnp.bfloat16), grad_block, preferred_element_type=jnp.float32
    )
    dprobs = jnp.einsum(
        "tngd,knd->tngk", grad_block, value_block, preferred_element_type=jnp.float32
    )
    dscores = (probs * (dprobs - delta[..., None])).astype(jnp.bfloat16)
    query_add = jnp.einsum("tngk,knd->tngd", dscores, key_block, preferred_element_type=jnp.float32)
    key_add = jnp.einsum("tngk,tngd->knd", dscores, query_block, preferred_element_type=jnp.float32)
    return (query_add, key_add, value_add)


def body(queries, key_proj, value_proj, out_grad, tile_order, doc_tiles):
    key_rows, value_rows = (
        lax.all_to_all(key_proj, "head", split_axis=1, concat_axis=0, tiled=True),
        lax.all_to_all(value_proj, "head", split_axis=1, concat_axis=0, tiled=True),
    )
    row_count = queries.shape[0]
    kv_local = key_rows.shape[1]
    group_size = queries.shape[1] // kv_local
    depth = queries.shape[2]
    query_rows = queries.reshape(row_count, kv_local, group_size, depth)
    grad_rows = out_grad.reshape(row_count, kv_local, group_size, depth)
    score_scale = 1.0 / math.sqrt(depth)
    cycle_size = lax.axis_size("ctx")
    my_shard = lax.axis_index("ctx")
    doc_ends = jnp.cumsum(doc_tiles)
    query_pos, query_doc, query_tiles, query_tdoc = row_info(
        tile_order, doc_ends, my_shard, row_count, TILE
    )

    def block_mask(shard):
        key_pos, key_doc, key_tiles, key_tdoc = row_info(
            tile_order, doc_ends, shard, row_count, TILE
        )
        allowed = (query_doc[:, None] == key_doc[None, :]) & (
            key_pos[None, :] <= query_pos[:, None]
        )
        reached = jnp.any(
            (query_tdoc[:, None] == key_tdoc[None, :])
            & (key_tiles[None, :] <= query_tiles[:, None])
        )
        return (allowed, reached)

    def forward_step(carried, key_block, value_block, shard):
        allowed, reached = block_mask(shard)
        return forward_block(carried, query_rows, key_block, value_block, allowed, score_scale)

    stats_shape = (row_count, kv_local, group_size)
    initial = (
        jnp.full(stats_shape, NEG, jnp.float32),
        jnp.zeros(stats_shape, jnp.float32),
        jnp.zeros(stats_shape + (depth,), jnp.float32),
    )
    first = forward_step(initial, key_rows, value_rows, my_shard)

    def forward_turn(turn_index, carried):
        key_block, value_block = from_behind((carried[0], carried[1]), "ctx", 1)
        shard = (my_shard - turn_index) % cycle_size
        return (key_block, value_block, forward_step(carried[2], key_block, value_block, shard))

    finished = lax.fori_loop(1, cycle_size, forward_turn, (key_rows, value_rows, first))
    running_max, running_sum, accumulated = finished[2]
    attended = (accumulated / running_sum[..., None]).astype(jnp.bfloat16)
    log_sum = running_max + jnp.log(running_sum)
    delta = jnp.sum(grad_rows.astype(jnp.float32) * attended.astype(jnp.float32), axis=-1)

    def backward_step(key_block, value_block, shard):
        allowed, reached = block_mask(shard)
        return backward_block(
            query_rows, grad_rows, log_sum, delta, key_block, value_block, allowed, score_scale
        )

    query_acc = jnp.zeros(stats_shape + (depth,), jnp.float32)

    def backward_turn(turn_index, carried):
        key_block, value_block, key_acc, value_acc, query_sum = carried
        shard = (my_shard - turn_index) % cycle_size
        query_add, key_add, value_add = backward_step(key_block, value_block, shard)
        key_block, value_block = from_behind((key_block, value_block), "ctx", 1)
        key_acc, value_acc = (
            from_behind((key_acc + key_add).astype(jnp.bfloat16), "ctx", 1).astype(jnp.float32),
            from_behind((value_acc + value_add).astype(jnp.bfloat16), "ctx", 1).astype(jnp.float32),
        )
        return (key_block, value_block, key_acc, value_acc, query_sum + query_add)

    grad_zero = jnp.zeros((row_count, kv_local, depth), jnp.float32)
    finished = lax.fori_loop(
        0, cycle_size, backward_turn, (key_rows, value_rows, grad_zero, grad_zero, query_acc)
    )
    key_acc, value_acc, query_acc = (finished[2], finished[3], finished[4])
    query_grad = (
        (query_acc * score_scale)
        .astype(jnp.bfloat16)
        .reshape(row_count, kv_local * group_size, depth)
    )
    key_grad = (key_acc * score_scale).astype(jnp.bfloat16)
    value_grad = value_acc.astype(jnp.bfloat16)
    attended = attended.reshape(row_count, kv_local * group_size, depth)
    key_back, value_back = (
        lax.all_to_all(key_grad, "head", split_axis=0, concat_axis=1, tiled=True),
        lax.all_to_all(value_grad, "head", split_axis=0, concat_axis=1, tiled=True),
    )
    return (attended, query_grad, key_back, value_back)


def solution(mesh):
    in_specs = (
        P("ctx", "head", None),
        P(("ctx", "head"), None, None),
        P(("ctx", "head"), None, None),
        P("ctx", "head", None),
        P(),
        P(),
    )
    out_specs = (
        P("ctx", "head", None),
        P("ctx", "head", None),
        P(("ctx", "head"), None, None),
        P(("ctx", "head"), None, None),
    )
    return jax.shard_map(body, mesh=mesh, in_specs=in_specs, out_specs=out_specs, check_vma=False)
```

profile of v0, /device:TPU:0, one launch (start us, length us, event | category | flops | bytes accessed | tf_op | source)
XLA Modules:
  0.0 183.4 jit_solution(8842191101418843890)
XLA Ops:
  0.6 1.5 copy.74
  2.2 5.2 %all-to-all-start = ((bf16[64,4,128]{2,0,1:T(8,128)(2,1)}), bf16[64,4,128]{2,0,1:T(8,128)(2,1)S(1)}, u32[]{:S(2)}, u32[]{:S(2)}) async-start(bf16[64,4,128]{2,0,1:T(8,128)(2,1)} %copy.74), calls=%async_computation | async-start | bytes 131072 | tf_op jit(solution)/shard_map/all_to_all | solution.py:73
  9.6 1.5 copy.75
  11.1 1.1 all-to-all-done
  12.2 3.3 %all-to-all-start.1 = ((bf16[64,4,128]{2,0,1:T(8,128)(2,1)}), bf16[64,4,128]{2,0,1:T(8,128)(2,1)S(1)}, u32[]{:S(2)}, u32[]{:S(2)}) async-start(bf16[64,4,128]{2,0,1:T(8,128)(2,1)} %copy.75), calls=%async_computation.1 | async-start | bytes 131072 | tf_op jit(solution)/shard_map/all_to_all | solution.py:74
  15.7 1.1 copy.107
  16.8 1.1 copy.81
  18.5 1.8 all-to-all-done.1
  21.9 0.9 fusion.52
  22.9 62.3 %while.48 = (s32[]{:T(128)}, bf16[256,1,128]{2,0,1:T(8,128)(2,1)}, bf16[256,1,128]{2,0,1:T(8,128)(2,1)}, f32[256,1,8]{0,2,1:T(8,128)S(1)}, f32[256,1,8]{0,2,1:T(...) while((s32[]{:T(128)}, bf16[256,1,128]{2,0,1:T(8,128)(2,1)}, ...), condition=%wide.region_8.9_spmd.clone, body=%wide.region_4.0_spmd.clone.sunk | while | flops 274930240 | bytes 10232312 | solution.py:120
  22.9 1.7 collective-permute-start.1
  24.6 1.3 add_bitcast_fusion.9
  30.9 0.9 fusion.101
  31.8 1.5 collective-permute-start.1
  33.3 1.3 add_bitcast_fusion.9
  39.8 0.9 fusion.101
  40.7 1.3 collective-permute-start.1
  42.0 1.3 add_bitcast_fusion.9
  48.7 0.9 fusion.101
  49.7 1.3 add_bitcast_fusion.9
  53.5 1.8 collective-permute-done
  57.6 0.9 fusion.101
  58.6 1.3 add_bitcast_fusion.9
  62.4 1.8 collective-permute-done
  66.5 0.9 fusion.101
  67.5 1.3 add_bitcast_fusion.9
  71.3 1.8 collective-permute-done
  75.4 0.9 fusion.101
  76.4 1.3 add_bitcast_fusion.9
  80.2 1.8 collective-permute-done
  84.3 0.9 fusion.101
  86.6 3.3 %multiply_reduce_fusion = (f32[256,8]{1,0:T(8,128)}, bf16[256,1,8,128]{3,2,0,1:T(8,128)(2,1)}) fusion(bf16[256,8,128]{2,1,0:T(8,128)(2,1)} %param.13, f32[256,8]{1,0:T(8,128)} %copy.79, f32[256,1,8,128]{3,0,2,1:T(8,128)S(1)} %get-tuple-element.648), kind=kLoop, calls=%fused_computation.83 | loop fusion | flops 1570816 | bytes 2113536 | tf_op jit(solution)/shard_map/reduce_sum | solution.py:124
  89.9 1.0 copy.82
  90.9 73.6 %while.49 = (s32[]{:T(128)}, bf16[256,1,128]{2,0,1:T(8,128)(2,1)S(1)}, bf16[256,1,128]{2,0,1:T(8,128)(2,1)S(1)}, f32[256,1,128]{2,0,1:T(8,128)S(1)}, f32[256,1,1...) while((s32[]{:T(128)}, ...), condition=%wide.region_12.13_spmd.clone, body=%wide.region_10.12_spmd.clone.sunk | while | flops 675742272 | bytes 16081516 | solution.py:146
  91.7 1.3 bitcast_select_fusion.4
  94.4 1.6 collective-permute-start.5
  96.8 2.6 %collective-permute-done.4 = bf16[256,1,128]{2,0,1:T(8,128)(2,1)S(1)} collective-permute-done((bf16[256,1,128]{2,0,1:T(8,128)(2,1)S(1)}, bf16[256,1,128]{2,0,1:T(8,128)(2,1)S(1)}, u32[]{:S(2)}, u32[]{:S(2)}) %collective-permute-start.4) | collective-permute-done | bytes 65568 | tf_op jit(solution)/shard_map/while/body/eval_jaxpr/ppermute | solution.py:14
  100.9 1.3 bitcast_select_fusion.4
  103.6 1.6 collective-permute-start.5
  105.1 0.9 fusion.116
  106.0 2.6 %collective-permute-done.4 = bf16[256,1,128]{2,0,1:T(8,128)(2,1)S(1)} collective-permute-done((bf16[256,1,128]{2,0,1:T(8,128)(2,1)S(1)}, bf16[256,1,128]{2,0,1:T(8,128)(2,1)S(1)}, u32[]{:S(2)}, u32[]{:S(2)}) %collective-permute-start.4) | collective-permute-done | bytes 65568 | tf_op jit(solution)/shard_map/while/body/eval_jaxpr/ppermute | solution.py:14
  110.1 1.3 bitcast_select_fusion.4
  112.8 1.5 collective-permute-start.5
  115.2 2.6 %collective-permute-done.4 = bf16[256,1,128]{2,0,1:T(8,128)(2,1)S(1)} collective-permute-done((bf16[256,1,128]{2,0,1:T(8,128)(2,1)S(1)}, bf16[256,1,128]{2,0,1:T(8,128)(2,1)S(1)}, u32[]{:S(2)}, u32[]{:S(2)}) %collective-permute-start.4) | collective-permute-done | bytes 65568 | tf_op jit(solution)/shard_map/while/body/eval_jaxpr/ppermute | solution.py:14
  119.3 1.3 bitcast_select_fusion.4
  122.0 1.5 collective-permute-start.5
  124.4 2.6 %collective-permute-done.4 = bf16[256,1,128]{2,0,1:T(8,128)(2,1)S(1)} collective-permute-done((bf16[256,1,128]{2,0,1:T(8,128)(2,1)S(1)}, bf16[256,1,128]{2,0,1:T(8,128)(2,1)S(1)}, u32[]{:S(2)}, u32[]{:S(2)}) %collective-permute-start.4) | collective-permute-done | bytes 65568 | tf_op jit(solution)/shard_map/while/body/eval_jaxpr/ppermute | solution.py:14
  128.5 1.3 bitcast_select_fusion.4
  131.2 1.5 collective-permute-start.5
  133.6 2.6 %collective-permute-done.4 = bf16[256,1,128]{2,0,1:T(8,128)(2,1)S(1)} collective-permute-done((bf16[256,1,128]{2,0,1:T(8,128)(2,1)S(1)}, bf16[256,1,128]{2,0,1:T(8,128)(2,1)S(1)}, u32[]{:S(2)}, u32[]{:S(2)}) %collective-permute-start.4) | collective-permute-done | bytes 65568 | tf_op jit(solution)/shard_map/while/body/eval_jaxpr/ppermute | solution.py:14
  137.7 1.3 bitcast_select_fusion.4
  140.4 1.5 collective-permute-start.5
  142.8 2.6 %collective-permute-done.4 = bf16[256,1,128]{2,0,1:T(8,128)(2,1)S(1)} collective-permute-done((bf16[256,1,128]{2,0,1:T(8,128)(2,1)S(1)}, bf16[256,1,128]{2,0,1:T(8,128)(2,1)S(1)}, u32[]{:S(2)}, u32[]{:S(2)}) %collective-permute-start.4) | collective-permute-done | bytes 65568 | tf_op jit(solution)/shard_map/while/body/eval_jaxpr/ppermute | solution.py:14
  146.9 1.3 bitcast_select_fusion.4
  149.6 1.5 collective-permute-start.5
  152.0 2.6 %collective-permute-done.4 = bf16[256,1,128]{2,0,1:T(8,128)(2,1)S(1)} collective-permute-done((bf16[256,1,128]{2,0,1:T(8,128)(2,1)S(1)}, bf16[256,1,128]{2,0,1:T(8,128)(2,1)S(1)}, u32[]{:S(2)}, u32[]{:S(2)}) %collective-permute-start.4) | collective-permute-done | bytes 65568 | tf_op jit(solution)/shard_map/while/body/eval_jaxpr/ppermute | solution.py:14
  156.1 1.3 bitcast_select_fusion.4
  158.8 1.5 collective-permute-start.5
  161.2 2.6 %collective-permute-done.4 = bf16[256,1,128]{2,0,1:T(8,128)(2,1)S(1)} collective-permute-done((bf16[256,1,128]{2,0,1:T(8,128)(2,1)S(1)}, bf16[256,1,128]{2,0,1:T(8,128)(2,1)S(1)}, u32[]{:S(2)}, u32[]{:S(2)}) %collective-permute-start.4) | collective-permute-done | bytes 65568 | tf_op jit(solution)/shard_map/while/body/eval_jaxpr/ppermute | solution.py:14
  166.4 3.3 %all-to-all-start.2 = ((bf16[4,2,4096]{2,1,0:T(2,128)(2,1)}), bf16[4,2,4096]{2,1,0:T(2,128)(2,1)S(1)}, u32[]{:S(2)}, u32[]{:S(2)}) async-start(bf16[4,2,4096]{2,1,0:T(2,128)(2,1)} %reshape.646), calls=%async_computation.2 | async-start | bytes 131072 | tf_op jit(solution)/shard_map/all_to_all | solution.py:159
  171.1 3.5 %all-to-all-done.2 = bf16[4,2,4096]{2,1,0:T(2,128)(2,1)S(1)} async-done(((bf16[4,2,4096]{2,1,0:T(2,128)(2,1)}), bf16[4,2,4096]{2,1,0:T(2,128)(2,1)S(1)}, u32[]{:S(2)}, u32[]{:S(2)}) %all-to-all-start.2) | async-done | bytes 65568 | tf_op jit(solution)/shard_map/all_to_all | solution.py:159
  174.5 3.3 %all-to-all-start.3 = ((bf16[4,2,4096]{2,1,0:T(2,128)(2,1)}), bf16[4,2,4096]{2,1,0:T(2,128)(2,1)S(1)}, u32[]{:S(2)}, u32[]{:S(2)}) async-start(bf16[4,2,4096]{2,1,0:T(2,128)(2,1)} %reshape.648), calls=%async_computation.3 | async-start | bytes 131072 | tf_op jit(solution)/shard_map/all_to_all | solution.py:160
  177.8 1.5 fusion.61
  180.1 2.6 %all-to-all-done.3 = bf16[4,2,4096]{2,1,0:T(2,128)(2,1)S(1)} async-done(((bf16[4,2,4096]{2,1,0:T(2,128)(2,1)}), bf16[4,2,4096]{2,1,0:T(2,128)(2,1)S(1)}, u32[]{:S(2)}, u32[]{:S(2)}) %all-to-all-start.3) | async-done | bytes 65568 | tf_op jit(solution)/shard_map/all_to_all | solution.py:160
  (302 shorter events, 73.5 us)
Async XLA Ops:
  0.6 20.3 %copy-start.4 = (bf16[256,8,128]{2,1,0:T(8,128)(2,1)S(1)}, bf16[256,8,128]{2,1,0:T(8,128)(2,1)}, u32[]{:S(2)}) copy-start(bf16[256,8,128]{2,1,0:T(8,128)(2,1)} %param.10) | copy-start | bytes 1572868
  2.2 10.0 %all-to-all-start = ((bf16[64,4,128]{2,0,1:T(8,128)(2,1)}), bf16[64,4,128]{2,0,1:T(8,128)(2,1)S(1)}, u32[]{:S(2)}, u32[]{:S(2)}) async-start(bf16[64,4,128]{2,0,1:T(8,128)(2,1)} %copy.74), calls=%async_computation | async-start | bytes 131072 | tf_op jit(solution)/shard_map/all_to_all | solution.py:73
  8.2 8.6 %copy-start.10 = (s32[4,1]{0,1:T(1,128)}, s32[4,1]{0,1:T(1,128)S(1)}, u32[]{:S(2)}) copy-start(s32[4,1]{0,1:T(1,128)S(1)} %reduce-window.8) | copy-start | bytes 52
  8.9 0.6 copy-start.5
  9.1 0.5 copy-start.8
  12.2 9.3 %copy-start = (bf16[64,4,128]{2,0,1:T(8,128)(2,1)}, bf16[64,4,128]{2,0,1:T(8,128)(2,1)S(1)}, u32[]{:S(2)}) copy-start(bf16[64,4,128]{2,0,1:T(8,128)(2,1)S(1)} %all-to-all-done) | copy-start | bytes 196612
  12.2 8.1 %all-to-all-start.1 = ((bf16[64,4,128]{2,0,1:T(8,128)(2,1)}), bf16[64,4,128]{2,0,1:T(8,128)(2,1)S(1)}, u32[]{:S(2)}, u32[]{:S(2)}) async-start(bf16[64,4,128]{2,0,1:T(8,128)(2,1)} %copy.75), calls=%async_computation.1 | async-start | bytes 131072 | tf_op jit(solution)/shard_map/all_to_all | solution.py:74
  20.3 1.6 copy-start.2
  22.9 5.8 %collective-permute-start = (bf16[256,1,128]{2,0,1:T(8,128)(2,1)}, bf16[256,1,128]{2,0,1:T(8,128)(2,1)S(1)}, u32[]{:S(2)}, u32[]{:S(2)}) collective-permute-start(bf16[256,1,128]{2,0,1:T(8,128)(2,1)} %get-tuple-element.1124), channel_id=1, source_target_pairs={{0,4},{4,8},{8,12},{12,16},{16,20},{20,24},{24,28},{28,0},{1,5},{5... | collective-permute-start | bytes 196616 | tf_op jit(solution)/shard_map/while/body/eval_jaxpr/ppermute | solution.py:14
  22.9 7.3 %collective-permute-start.1 = (bf16[256,1,128]{2,0,1:T(8,128)(2,1)}, bf16[256,1,128]{2,0,1:T(8,128)(2,1)S(1)}, u32[]{:S(2)}, u32[]{:S(2)}) collective-permute-start(bf16[256,1,128]{2,0,1:T(8,128)(2,1)} %get-tuple-element.1125), channel_id=1, source_target_pairs={{0,4},{4,8},{8,12},{12,16},{16,20},{20,24},{24,28},{28,0},{1,5},{5... | collective-permute-start | bytes 196616 | tf_op jit(solution)/shard_map/while/body/eval_jaxpr/ppermute | solution.py:14
  31.8 5.8 %collective-permute-start = (bf16[256,1,128]{2,0,1:T(8,128)(2,1)}, bf16[256,1,128]{2,0,1:T(8,128)(2,1)S(1)}, u32[]{:S(2)}, u32[]{:S(2)}) collective-permute-start(bf16[256,1,128]{2,0,1:T(8,128)(2,1)} %get-tuple-element.1124), channel_id=1, source_target_pairs={{0,4},{4,8},{8,12},{12,16},{16,20},{20,24},{24,28},{28,0},{1,5},{5... | collective-permute-start | bytes 196616 | tf_op jit(solution)/shard_map/while/body/eval_jaxpr/ppermute | solution.py:14
  31.8 7.3 %collective-permute-start.1 = (bf16[256,1,128]{2,0,1:T(8,128)(2,1)}, bf16[256,1,128]{2,0,1:T(8,128)(2,1)S(1)}, u32[]{:S(2)}, u32[]{:S(2)}) collective-permute-start(bf16[256,1,128]{2,0,1:T(8,128)(2,1)} %get-tuple-element.1125), channel_id=1, source_target_pairs={{0,4},{4,8},{8,12},{12,16},{16,20},{20,24},{24,28},{28,0},{1,5},{5... | collective-permute-start | bytes 196616 | tf_op jit(solution)/shard_map/while/body/eval_jaxpr/ppermute | solution.py:14
  40.7 5.8 %collective-permute-start = (bf16[256,1,128]{2,0,1:T(8,128)(2,1)}, bf16[256,1,128]{2,0,1:T(8,128)(2,1)S(1)}, u32[]{:S(2)}, u32[]{:S(2)}) collective-permute-start(bf16[256,1,128]{2,0,1:T(8,128)(2,1)} %get-tuple-element.1124), channel_id=1, source_target_pairs={{0,4},{4,8},{8,12},{12,16},{16,20},{20,24},{24,28},{28,0},{1,5},{5... | collective-permute-start | bytes 196616 | tf_op jit(solution)/shard_map/while/body/eval_jaxpr/ppermute | solution.py:14
  40.7 7.3 %collective-permute-start.1 = (bf16[256,1,128]{2,0,1:T(8,128)(2,1)}, bf16[256,1,128]{2,0,1:T(8,128)(2,1)S(1)}, u32[]{:S(2)}, u32[]{:S(2)}) collective-permute-start(bf16[256,1,128]{2,0,1:T(8,128)(2,1)} %get-tuple-element.1125), channel_id=1, source_target_pairs={{0,4},{4,8},{8,12},{12,16},{16,20},{20,24},{24,28},{28,0},{1,5},{5... | collective-permute-start | bytes 196616 | tf_op jit(solution)/shard_map/while/body/eval_jaxpr/ppermute | solution.py:14
  49.6 5.8 %collective-permute-start = (bf16[256,1,128]{2,0,1:T(8,128)(2,1)}, bf16[256,1,128]{2,0,1:T(8,128)(2,1)S(1)}, u32[]{:S(2)}, u32[]{:S(2)}) collective-permute-start(bf16[256,1,128]{2,0,1:T(8,128)(2,1)} %get-tuple-element.1124), channel_id=1, source_target_pairs={{0,4},{4,8},{8,12},{12,16},{16,20},{20,24},{24,28},{28,0},{1,5},{5... | collective-permute-start | bytes 196616 | tf_op jit(solution)/shard_map/while/body/eval_jaxpr/ppermute | solution.py:14
  49.6 7.3 %collective-permute-start.1 = (bf16[256,1,128]{2,0,1:T(8,128)(2,1)}, bf16[256,1,128]{2,0,1:T(8,128)(2,1)S(1)}, u32[]{:S(2)}, u32[]{:S(2)}) collective-permute-start(bf16[256,1,128]{2,0,1:T(8,128)(2,1)} %get-tuple-element.1125), channel_id=1, source_target_pairs={{0,4},{4,8},{8,12},{12,16},{16,20},{20,24},{24,28},{28,0},{1,5},{5... | collective-permute-start | bytes 196616 | tf_op jit(solution)/shard_map/while/body/eval_jaxpr/ppermute | solution.py:14
  58.5 5.8 %collective-permute-start = (bf16[256,1,128]{2,0,1:T(8,128)(2,1)}, bf16[256,1,128]{2,0,1:T(8,128)(2,1)S(1)}, u32[]{:S(2)}, u32[]{:S(2)}) collective-permute-start(bf16[256,1,128]{2,0,1:T(8,128)(2,1)} %get-tuple-element.1124), channel_id=1, source_target_pairs={{0,4},{4,8},{8,12},{12,16},{16,20},{20,24},{24,28},{28,0},{1,5},{5... | collective-permute-start | bytes 196616 | tf_op jit(solution)/shard_map/while/body/eval_jaxpr/ppermute | solution.py:14
  58.5 7.3 %collective-permute-start.1 = (bf16[256,1,128]{2,0,1:T(8,128)(2,1)}, bf16[256,1,128]{2,0,1:T(8,128)(2,1)S(1)}, u32[]{:S(2)}, u32[]{:S(2)}) collective-permute-start(bf16[256,1,128]{2,0,1:T(8,128)(2,1)} %get-tuple-element.1125), channel_id=1, source_target_pairs={{0,4},{4,8},{8,12},{12,16},{16,20},{20,24},{24,28},{28,0},{1,5},{5... | collective-permute-start | bytes 196616 | tf_op jit(solution)/shard_map/while/body/eval_jaxpr/ppermute | solution.py:14
  67.4 5.8 %collective-permute-start = (bf16[256,1,128]{2,0,1:T(8,128)(2,1)}, bf16[256,1,128]{2,0,1:T(8,128)(2,1)S(1)}, u32[]{:S(2)}, u32[]{:S(2)}) collective-permute-start(bf16[256,1,128]{2,0,1:T(8,128)(2,1)} %get-tuple-element.1124), channel_id=1, source_target_pairs={{0,4},{4,8},{8,12},{12,16},{16,20},{20,24},{24,28},{28,0},{1,5},{5... | collective-permute-start | bytes 196616 | tf_op jit(solution)/shard_map/while/body/eval_jaxpr/ppermute | solution.py:14
  67.4 7.3 %collective-permute-start.1 = (bf16[256,1,128]{2,0,1:T(8,128)(2,1)}, bf16[256,1,128]{2,0,1:T(8,128)(2,1)S(1)}, u32[]{:S(2)}, u32[]{:S(2)}) collective-permute-start(bf16[256,1,128]{2,0,1:T(8,128)(2,1)} %get-tuple-element.1125), channel_id=1, source_target_pairs={{0,4},{4,8},{8,12},{12,16},{16,20},{20,24},{24,28},{28,0},{1,5},{5... | collective-permute-start | bytes 196616 | tf_op jit(solution)/shard_map/while/body/eval_jaxpr/ppermute | solution.py:14
  76.3 5.8 %collective-permute-start = (bf16[256,1,128]{2,0,1:T(8,128)(2,1)}, bf16[256,1,128]{2,0,1:T(8,128)(2,1)S(1)}, u32[]{:S(2)}, u32[]{:S(2)}) collective-permute-start(bf16[256,1,128]{2,0,1:T(8,128)(2,1)} %get-tuple-element.1124), channel_id=1, source_target_pairs={{0,4},{4,8},{8,12},{12,16},{16,20},{20,24},{24,28},{28,0},{1,5},{5... | collective-permute-start | bytes 196616 | tf_op jit(solution)/shard_map/while/body/eval_jaxpr/ppermute | solution.py:14
  76.3 7.3 %collective-permute-start.1 = (bf16[256,1,128]{2,0,1:T(8,128)(2,1)}, bf16[256,1,128]{2,0,1:T(8,128)(2,1)S(1)}, u32[]{:S(2)}, u32[]{:S(2)}) collective-permute-start(bf16[256,1,128]{2,0,1:T(8,128)(2,1)} %get-tuple-element.1125), channel_id=1, source_target_pairs={{0,4},{4,8},{8,12},{12,16},{16,20},{20,24},{24,28},{28,0},{1,5},{5... | collective-permute-start | bytes 196616 | tf_op jit(solution)/shard_map/while/body/eval_jaxpr/ppermute | solution.py:14
  85.2 5.7 %copy-start.1 = (bf16[64,4,128]{2,0,1:T(8,128)(2,1)S(1)}, bf16[64,4,128]{2,0,1:T(8,128)(2,1)}, u32[]{:S(2)}) copy-start(bf16[64,4,128]{2,0,1:T(8,128)(2,1)} %copy-done) | copy-start | bytes 196612
  85.2 5.7 %copy-start.3 = (bf16[64,4,128]{2,0,1:T(8,128)(2,1)S(1)}, bf16[64,4,128]{2,0,1:T(8,128)(2,1)}, u32[]{:S(2)}) copy-start(bf16[64,4,128]{2,0,1:T(8,128)(2,1)} %copy-done.2) | copy-start | bytes 196612
  86.6 4.3 %copy-start.6 = (s32[2]{0:T(128)S(1)}, s32[2]{0:T(128)}, u32[]{:S(2)}) copy-start(s32[2]{0:T(128)} %get-tuple-element.1237) | copy-start | bytes 28
  86.6 4.3 %copy-start.7 = (s32[16]{0:T(128)S(1)}, s32[16]{0:T(128)}, u32[]{:S(2)}) copy-start(s32[16]{0:T(128)} %get-tuple-element.1240) | copy-start | bytes 196
  86.6 4.3 %copy-start.9 = (s32[2]{0:T(128)S(1)}, s32[2]{0:T(128)}, u32[]{:S(2)}) copy-start(s32[2]{0:T(128)} %get-tuple-element.1241) | copy-start | bytes 28
  86.6 4.3 %copy-start.11 = (s32[4]{0:T(128)S(1)}, s32[4]{0:T(128)}, u32[]{:S(2)}) copy-start(s32[4]{0:T(128)} %get-tuple-element.1242) | copy-start | bytes 52
  91.0 9.2 %collective-permute-start.2 = (bf16[256,1,128]{2,0,1:T(8,128)(2,1)S(1)}, bf16[256,1,128]{2,0,1:T(8,128)(2,1)S(1)}, u32[]{:S(2)}, u32[]{:S(2)}) collective-permute-start(bf16[256,1,128]{2,0,1:T(8,128)(2,1)S(1)} %copy.135), channel_id=1, source_target_pairs={{0,4},{4,8},{8,12},{12,16},{16,20},{20,24},{24,28},{28,0},{1,5},{5... | collective-permute-start | bytes 196616 | tf_op jit(solution)/shard_map/while/body/eval_jaxpr/ppermute | solution.py:14
  91.0 9.1 %collective-permute-start.3 = (bf16[256,1,128]{2,0,1:T(8,128)(2,1)S(1)}, bf16[256,1,128]{2,0,1:T(8,128)(2,1)S(1)}, u32[]{:S(2)}, u32[]{:S(2)}) collective-permute-start(bf16[256,1,128]{2,0,1:T(8,128)(2,1)S(1)} %copy.136), channel_id=1, source_target_pairs={{0,4},{4,8},{8,12},{12,16},{16,20},{20,24},{24,28},{28,0},{1,5},{5... | collective-permute-start | bytes 196616 | tf_op jit(solution)/shard_map/while/body/eval_jaxpr/ppermute | solution.py:14
  93.9 5.5 %collective-permute-start.4 = (bf16[256,1,128]{2,0,1:T(8,128)(2,1)S(1)}, bf16[256,1,128]{2,0,1:T(8,128)(2,1)S(1)}, u32[]{:S(2)}, u32[]{:S(2)}) collective-permute-start(bf16[256,1,128]{2,0,1:T(8,128)(2,1)S(1)} %fusion.114), channel_id=1, source_target_pairs={{0,4},{4,8},{8,12},{12,16},{16,20},{20,24},{24,28},{28,0},{1,5},{5... | collective-permute-start | bytes 196616 | tf_op jit(solution)/shard_map/while/body/eval_jaxpr/ppermute | solution.py:14
  94.4 5.7 %collective-permute-start.5 = (bf16[256,1,128]{2,0,1:T(8,128)(2,1)S(1)}, bf16[256,1,128]{2,0,1:T(8,128)(2,1)S(1)}, u32[]{:S(2)}, u32[]{:S(2)}) collective-permute-start(bf16[256,1,128]{2,0,1:T(8,128)(2,1)S(1)} %fusion.115), channel_id=1, source_target_pairs={{0,4},{4,8},{8,12},{12,16},{16,20},{20,24},{24,28},{28,0},{1,5},{5... | collective-permute-start | bytes 196616 | tf_op jit(solution)/shard_map/while/body/eval_jaxpr/ppermute | solution.py:14
  100.2 9.2 %collective-permute-start.2 = (bf16[256,1,128]{2,0,1:T(8,128)(2,1)S(1)}, bf16[256,1,128]{2,0,1:T(8,128)(2,1)S(1)}, u32[]{:S(2)}, u32[]{:S(2)}) collective-permute-start(bf16[256,1,128]{2,0,1:T(8,128)(2,1)S(1)} %copy.135), channel_id=1, source_target_pairs={{0,4},{4,8},{8,12},{12,16},{16,20},{20,24},{24,28},{28,0},{1,5},{5... | collective-permute-start | bytes 196616 | tf_op jit(solution)/shard_map/while/body/eval_jaxpr/ppermute | solution.py:14
  100.3 9.1 %collective-permute-start.3 = (bf16[256,1,128]{2,0,1:T(8,128)(2,1)S(1)}, bf16[256,1,128]{2,0,1:T(8,128)(2,1)S(1)}, u32[]{:S(2)}, u32[]{:S(2)}) collective-permute-start(bf16[256,1,128]{2,0,1:T(8,128)(2,1)S(1)} %copy.136), channel_id=1, source_target_pairs={{0,4},{4,8},{8,12},{12,16},{16,20},{20,24},{24,28},{28,0},{1,5},{5... | collective-permute-start | bytes 196616 | tf_op jit(solution)/shard_map/while/body/eval_jaxpr/ppermute | solution.py:14
  103.1 5.5 %collective-permute-start.4 = (bf16[256,1,128]{2,0,1:T(8,128)(2,1)S(1)}, bf16[256,1,128]{2,0,1:T(8,128)(2,1)S(1)}, u32[]{:S(2)}, u32[]{:S(2)}) collective-permute-start(bf16[256,1,128]{2,0,1:T(8,128)(2,1)S(1)} %fusion.114), channel_id=1, source_target_pairs={{0,4},{4,8},{8,12},{12,16},{16,20},{20,24},{24,28},{28,0},{1,5},{5... | collective-permute-start | bytes 196616 | tf_op jit(solution)/shard_map/while/body/eval_jaxpr/ppermute | solution.py:14
  103.6 5.7 %collective-permute-start.5 = (bf16[256,1,128]{2,0,1:T(8,128)(2,1)S(1)}, bf16[256,1,128]{2,0,1:T(8,128)(2,1)S(1)}, u32[]{:S(2)}, u32[]{:S(2)}) collective-permute-start(bf16[256,1,128]{2,0,1:T(8,128)(2,1)S(1)} %fusion.115), channel_id=1, source_target_pairs={{0,4},{4,8},{8,12},{12,16},{16,20},{20,24},{24,28},{28,0},{1,5},{5... | collective-permute-start | bytes 196616 | tf_op jit(solution)/shard_map/while/body/eval_jaxpr/ppermute | solution.py:14
  109.4 9.2 %collective-permute-start.2 = (bf16[256,1,128]{2,0,1:T(8,128)(2,1)S(1)}, bf16[256,1,128]{2,0,1:T(8,128)(2,1)S(1)}, u32[]{:S(2)}, u32[]{:S(2)}) collective-permute-start(bf16[256,1,128]{2,0,1:T(8,128)(2,1)S(1)} %copy.135), channel_id=1, source_target_pairs={{0,4},{4,8},{8,12},{12,16},{16,20},{20,24},{24,28},{28,0},{1,5},{5... | collective-permute-start | bytes 196616 | tf_op jit(solution)/shard_map/while/body/eval_jaxpr/ppermute | solution.py:14
  109.5 9.1 %collective-permute-start.3 = (bf16[256,1,128]{2,0,1:T(8,128)(2,1)S(1)}, bf16[256,1,128]{2,0,1:T(8,128)(2,1)S(1)}, u32[]{:S(2)}, u32[]{:S(2)}) collective-permute-start(bf16[256,1,128]{2,0,1:T(8,128)(2,1)S(1)} %copy.136), channel_id=1, source_target_pairs={{0,4},{4,8},{8,12},{12,16},{16,20},{20,24},{24,28},{28,0},{1,5},{5... | collective-permute-start | bytes 196616 | tf_op jit(solution)/shard_map/while/body/eval_jaxpr/ppermute | solution.py:14
  112.3 5.5 %collective-permute-start.4 = (bf16[256,1,128]{2,0,1:T(8,128)(2,1)S(1)}, bf16[256,1,128]{2,0,1:T(8,128)(2,1)S(1)}, u32[]{:S(2)}, u32[]{:S(2)}) collective-permute-start(bf16[256,1,128]{2,0,1:T(8,128)(2,1)S(1)} %fusion.114), channel_id=1, source_target_pairs={{0,4},{4,8},{8,12},{12,16},{16,20},{20,24},{24,28},{28,0},{1,5},{5... | collective-permute-start | bytes 196616 | tf_op jit(solution)/shard_map/while/body/eval_jaxpr/ppermute | solution.py:14
  112.8 5.7 %collective-permute-start.5 = (bf16[256,1,128]{2,0,1:T(8,128)(2,1)S(1)}, bf16[256,1,128]{2,0,1:T(8,128)(2,1)S(1)}, u32[]{:S(2)}, u32[]{:S(2)}) collective-permute-start(bf16[256,1,128]{2,0,1:T(8,128)(2,1)S(1)} %fusion.115), channel_id=1, source_target_pairs={{0,4},{4,8},{8,12},{12,16},{16,20},{20,24},{24,28},{28,0},{1,5},{5... | collective-permute-start | bytes 196616 | tf_op jit(solution)/shard_map/while/body/eval_jaxpr/ppermute | solution.py:14
  118.6 9.2 %collective-permute-start.2 = (bf16[256,1,128]{2,0,1:T(8,128)(2,1)S(1)}, bf16[256,1,128]{2,0,1:T(8,128)(2,1)S(1)}, u32[]{:S(2)}, u32[]{:S(2)}) collective-permute-start(bf16[256,1,128]{2,0,1:T(8,128)(2,1)S(1)} %copy.135), channel_id=1, source_target_pairs={{0,4},{4,8},{8,12},{12,16},{16,20},{20,24},{24,28},{28,0},{1,5},{5... | collective-permute-start | bytes 196616 | tf_op jit(solution)/shard_map/while/body/eval_jaxpr/ppermute | solution.py:14
  118.7 9.1 %collective-permute-start.3 = (bf16[256,1,128]{2,0,1:T(8,128)(2,1)S(1)}, bf16[256,1,128]{2,0,1:T(8,128)(2,1)S(1)}, u32[]{:S(2)}, u32[]{:S(2)}) collective-permute-start(bf16[256,1,128]{2,0,1:T(8,128)(2,1)S(1)} %copy.136), channel_id=1, source_target_pairs={{0,4},{4,8},{8,12},{12,16},{16,20},{20,24},{24,28},{28,0},{1,5},{5... | collective-permute-start | bytes 196616 | tf_op jit(solution)/shard_map/while/body/eval_jaxpr/ppermute | solution.py:14
  121.5 5.5 %collective-permute-start.4 = (bf16[256,1,128]{2,0,1:T(8,128)(2,1)S(1)}, bf16[256,1,128]{2,0,1:T(8,128)(2,1)S(1)}, u32[]{:S(2)}, u32[]{:S(2)}) collective-permute-start(bf16[256,1,128]{2,0,1:T(8,128)(2,1)S(1)} %fusion.114), channel_id=1, source_target_pairs={{0,4},{4,8},{8,12},{12,16},{16,20},{20,24},{24,28},{28,0},{1,5},{5... | collective-permute-start | bytes 196616 | tf_op jit(solution)/shard_map/while/body/eval_jaxpr/ppermute | solution.py:14
  122.0 5.7 %collective-permute-start.5 = (bf16[256,1,128]{2,0,1:T(8,128)(2,1)S(1)}, bf16[256,1,128]{2,0,1:T(8,128)(2,1)S(1)}, u32[]{:S(2)}, u32[]{:S(2)}) collective-permute-start(bf16[256,1,128]{2,0,1:T(8,128)(2,1)S(1)} %fusion.115), channel_id=1, source_target_pairs={{0,4},{4,8},{8,12},{12,16},{16,20},{20,24},{24,28},{28,0},{1,5},{5... | collective-permute-start | bytes 196616 | tf_op jit(solution)/shard_map/while/body/eval_jaxpr/ppermute | solution.py:14
  127.8 9.2 %collective-permute-start.2 = (bf16[256,1,128]{2,0,1:T(8,128)(2,1)S(1)}, bf16[256,1,128]{2,0,1:T(8,128)(2,1)S(1)}, u32[]{:S(2)}, u32[]{:S(2)}) collective-permute-start(bf16[256,1,128]{2,0,1:T(8,128)(2,1)S(1)} %copy.135), channel_id=1, source_target_pairs={{0,4},{4,8},{8,12},{12,16},{16,20},{20,24},{24,28},{28,0},{1,5},{5... | collective-permute-start | bytes 196616 | tf_op jit(solution)/shard_map/while/body/eval_jaxpr/ppermute | solution.py:14
  127.9 9.1 %collective-permute-start.3 = (bf16[256,1,128]{2,0,1:T(8,128)(2,1)S(1)}, bf16[256,1,128]{2,0,1:T(8,128)(2,1)S(1)}, u32[]{:S(2)}, u32[]{:S(2)}) collective-permute-start(bf16[256,1,128]{2,0,1:T(8,128)(2,1)S(1)} %copy.136), channel_id=1, source_target_pairs={{0,4},{4,8},{8,12},{12,16},{16,20},{20,24},{24,28},{28,0},{1,5},{5... | collective-permute-start | bytes 196616 | tf_op jit(solution)/shard_map/while/body/eval_jaxpr/ppermute | solution.py:14
  130.7 5.5 %collective-permute-start.4 = (bf16[256,1,128]{2,0,1:T(8,128)(2,1)S(1)}, bf16[256,1,128]{2,0,1:T(8,128)(2,1)S(1)}, u32[]{:S(2)}, u32[]{:S(2)}) collective-permute-start(bf16[256,1,128]{2,0,1:T(8,128)(2,1)S(1)} %fusion.114), channel_id=1, source_target_pairs={{0,4},{4,8},{8,12},{12,16},{16,20},{20,24},{24,28},{28,0},{1,5},{5... | collective-permute-start | bytes 196616 | tf_op jit(solution)/shard_map/while/body/eval_jaxpr/ppermute | solution.py:14
  131.2 5.7 %collective-permute-start.5 = (bf16[256,1,128]{2,0,1:T(8,128)(2,1)S(1)}, bf16[256,1,128]{2,0,1:T(8,128)(2,1)S(1)}, u32[]{:S(2)}, u32[]{:S(2)}) collective-permute-start(bf16[256,1,128]{2,0,1:T(8,128)(2,1)S(1)} %fusion.115), channel_id=1, source_target_pairs={{0,4},{4,8},{8,12},{12,16},{16,20},{20,24},{24,28},{28,0},{1,5},{5... | collective-permute-start | bytes 196616 | tf_op jit(solution)/shard_map/while/body/eval_jaxpr/ppermute | solution.py:14
  137.0 9.2 %collective-permute-start.2 = (bf16[256,1,128]{2,0,1:T(8,128)(2,1)S(1)}, bf16[256,1,128]{2,0,1:T(8,128)(2,1)S(1)}, u32[]{:S(2)}, u32[]{:S(2)}) collective-permute-start(bf16[256,1,128]{2,0,1:T(8,128)(2,1)S(1)} %copy.135), channel_id=1, source_target_pairs={{0,4},{4,8},{8,12},{12,16},{16,20},{20,24},{24,28},{28,0},{1,5},{5... | collective-permute-start | bytes 196616 | tf_op jit(solution)/shard_map/while/body/eval_jaxpr/ppermute | solution.py:14
  137.1 9.1 %collective-permute-start.3 = (bf16[256,1,128]{2,0,1:T(8,128)(2,1)S(1)}, bf16[256,1,128]{2,0,1:T(8,128)(2,1)S(1)}, u32[]{:S(2)}, u32[]{:S(2)}) collective-permute-start(bf16[256,1,128]{2,0,1:T(8,128)(2,1)S(1)} %copy.136), channel_id=1, source_target_pairs={{0,4},{4,8},{8,12},{12,16},{16,20},{20,24},{24,28},{28,0},{1,5},{5... | collective-permute-start | bytes 196616 | tf_op jit(solution)/shard_map/while/body/eval_jaxpr/ppermute | solution.py:14
  139.9 5.5 %collective-permute-start.4 = (bf16[256,1,128]{2,0,1:T(8,128)(2,1)S(1)}, bf16[256,1,128]{2,0,1:T(8,128)(2,1)S(1)}, u32[]{:S(2)}, u32[]{:S(2)}) collective-permute-start(bf16[256,1,128]{2,0,1:T(8,128)(2,1)S(1)} %fusion.114), channel_id=1, source_target_pairs={{0,4},{4,8},{8,12},{12,16},{16,20},{20,24},{24,28},{28,0},{1,5},{5... | collective-permute-start | bytes 196616 | tf_op jit(solution)/shard_map/while/body/eval_jaxpr/ppermute | solution.py:14
  140.4 5.7 %collective-permute-start.5 = (bf16[256,1,128]{2,0,1:T(8,128)(2,1)S(1)}, bf16[256,1,128]{2,0,1:T(8,128)(2,1)S(1)}, u32[]{:S(2)}, u32[]{:S(2)}) collective-permute-start(bf16[256,1,128]{2,0,1:T(8,128)(2,1)S(1)} %fusion.115), channel_id=1, source_target_pairs={{0,4},{4,8},{8,12},{12,16},{16,20},{20,24},{24,28},{28,0},{1,5},{5... | collective-permute-start | bytes 196616 | tf_op jit(solution)/shard_map/while/body/eval_jaxpr/ppermute | solution.py:14
  146.2 9.2 %collective-permute-start.2 = (bf16[256,1,128]{2,0,1:T(8,128)(2,1)S(1)}, bf16[256,1,128]{2,0,1:T(8,128)(2,1)S(1)}, u32[]{:S(2)}, u32[]{:S(2)}) collective-permute-start(bf16[256,1,128]{2,0,1:T(8,128)(2,1)S(1)} %copy.135), channel_id=1, source_target_pairs={{0,4},{4,8},{8,12},{12,16},{16,20},{20,24},{24,28},{28,0},{1,5},{5... | collective-permute-start | bytes 196616 | tf_op jit(solution)/shard_map/while/body/eval_jaxpr/ppermute | solution.py:14
  146.3 9.1 %collective-permute-start.3 = (bf16[256,1,128]{2,0,1:T(8,128)(2,1)S(1)}, bf16[256,1,128]{2,0,1:T(8,128)(2,1)S(1)}, u32[]{:S(2)}, u32[]{:S(2)}) collective-permute-start(bf16[256,1,128]{2,0,1:T(8,128)(2,1)S(1)} %copy.136), channel_id=1, source_target_pairs={{0,4},{4,8},{8,12},{12,16},{16,20},{20,24},{24,28},{28,0},{1,5},{5... | collective-permute-start | bytes 196616 | tf_op jit(solution)/shard_map/while/body/eval_jaxpr/ppermute | solution.py:14
  149.1 5.5 %collective-permute-start.4 = (bf16[256,1,128]{2,0,1:T(8,128)(2,1)S(1)}, bf16[256,1,128]{2,0,1:T(8,128)(2,1)S(1)}, u32[]{:S(2)}, u32[]{:S(2)}) collective-permute-start(bf16[256,1,128]{2,0,1:T(8,128)(2,1)S(1)} %fusion.114), channel_id=1, source_target_pairs={{0,4},{4,8},{8,12},{12,16},{16,20},{20,24},{24,28},{28,0},{1,5},{5... | collective-permute-start | bytes 196616 | tf_op jit(solution)/shard_map/while/body/eval_jaxpr/ppermute | solution.py:14
  149.6 5.7 %collective-permute-start.5 = (bf16[256,1,128]{2,0,1:T(8,128)(2,1)S(1)}, bf16[256,1,128]{2,0,1:T(8,128)(2,1)S(1)}, u32[]{:S(2)}, u32[]{:S(2)}) collective-permute-start(bf16[256,1,128]{2,0,1:T(8,128)(2,1)S(1)} %fusion.115), channel_id=1, source_target_pairs={{0,4},{4,8},{8,12},{12,16},{16,20},{20,24},{24,28},{28,0},{1,5},{5... | collective-permute-start | bytes 196616 | tf_op jit(solution)/shard_map/while/body/eval_jaxpr/ppermute | solution.py:14
  155.4 9.2 %collective-permute-start.2 = (bf16[256,1,128]{2,0,1:T(8,128)(2,1)S(1)}, bf16[256,1,128]{2,0,1:T(8,128)(2,1)S(1)}, u32[]{:S(2)}, u32[]{:S(2)}) collective-permute-start(bf16[256,1,128]{2,0,1:T(8,128)(2,1)S(1)} %copy.135), channel_id=1, source_target_pairs={{0,4},{4,8},{8,12},{12,16},{16,20},{20,24},{24,28},{28,0},{1,5},{5... | collective-permute-start | bytes 196616 | tf_op jit(solution)/shard_map/while/body/eval_jaxpr/ppermute | solution.py:14
  155.5 9.1 %collective-permute-start.3 = (bf16[256,1,128]{2,0,1:T(8,128)(2,1)S(1)}, bf16[256,1,128]{2,0,1:T(8,128)(2,1)S(1)}, u32[]{:S(2)}, u32[]{:S(2)}) collective-permute-start(bf16[256,1,128]{2,0,1:T(8,128)(2,1)S(1)} %copy.136), channel_id=1, source_target_pairs={{0,4},{4,8},{8,12},{12,16},{16,20},{20,24},{24,28},{28,0},{1,5},{5... | collective-permute-start | bytes 196616 | tf_op jit(solution)/shard_map/while/body/eval_jaxpr/ppermute | solution.py:14
  158.3 5.5 %collective-permute-start.4 = (bf16[256,1,128]{2,0,1:T(8,128)(2,1)S(1)}, bf16[256,1,128]{2,0,1:T(8,128)(2,1)S(1)}, u32[]{:S(2)}, u32[]{:S(2)}) collective-permute-start(bf16[256,1,128]{2,0,1:T(8,128)(2,1)S(1)} %fusion.114), channel_id=1, source_target_pairs={{0,4},{4,8},{8,12},{12,16},{16,20},{20,24},{24,28},{28,0},{1,5},{5... | collective-permute-start | bytes 196616 | tf_op jit(solution)/shard_map/while/body/eval_jaxpr/ppermute | solution.py:14
  158.8 5.7 %collective-permute-start.5 = (bf16[256,1,128]{2,0,1:T(8,128)(2,1)S(1)}, bf16[256,1,128]{2,0,1:T(8,128)(2,1)S(1)}, u32[]{:S(2)}, u32[]{:S(2)}) collective-permute-start(bf16[256,1,128]{2,0,1:T(8,128)(2,1)S(1)} %fusion.115), channel_id=1, source_target_pairs={{0,4},{4,8},{8,12},{12,16},{16,20},{20,24},{24,28},{28,0},{1,5},{5... | collective-permute-start | bytes 196616 | tf_op jit(solution)/shard_map/while/body/eval_jaxpr/ppermute | solution.py:14
  166.4 8.1 %all-to-all-start.2 = ((bf16[4,2,4096]{2,1,0:T(2,128)(2,1)}), bf16[4,2,4096]{2,1,0:T(2,128)(2,1)S(1)}, u32[]{:S(2)}, u32[]{:S(2)}) async-start(bf16[4,2,4096]{2,1,0:T(2,128)(2,1)} %reshape.646), calls=%async_computation.2 | async-start | bytes 131072 | tf_op jit(solution)/shard_map/all_to_all | solution.py:159
  174.5 8.1 %all-to-all-start.3 = ((bf16[4,2,4096]{2,1,0:T(2,128)(2,1)}), bf16[4,2,4096]{2,1,0:T(2,128)(2,1)S(1)}, u32[]{:S(2)}, u32[]{:S(2)}) async-start(bf16[4,2,4096]{2,1,0:T(2,128)(2,1)} %reshape.648), calls=%async_computation.3 | async-start | bytes 131072 | tf_op jit(solution)/shard_map/all_to_all | solution.py:160
where the time goes:
time: 185 us; the launch traced here: 183 us
  waiting for transfers between devices  43.8 us (24%)
  other arithmetic  43.5 us (24%)
  matrix products  38.5 us (21%)
  starting transfers between devices  33.8 us (18%)
  local copies, waits for them, and re-layouts  21 us (11%)
    ppermute x46, waiting for transfers between devices, from_behind(): return lax.ppermute(value, axis, pairs)  34.9 us
    ppermute x46, starting transfers between devices, from_behind(): return lax.ppermute(value, axis, pairs)  18.8 us
    dot_general x16, matrix products, block_scores(): jnp.einsum('tngd,knd->tngk', query_block, key_block, preferred_element_ty...  13.9 us
    unnamed x39, local copies, waits for them, and re-layouts  10.8 us
    le x15, other arithmetic, block_mask(): key_pos[None, :] <= query_pos[:, None]  9.68 us
    while x37, local copies, waits for them, and re-layouts  8.95 us
    reduce_sum x16, other arithmetic, row_info(): jnp.sum((shard_tiles[:, None] >= doc_ends[None, :]).astype(jnp.int32), ax...  7.69 us
    dot_general x8, matrix products, forward_block(): jnp.einsum('tngk,knd->tngd', weights.astype(jnp.bfloat16), value_block, p...  7.21 us
  transfers between devices with their start and end apart: 50, of which 27 were waited for; matrix products, arithmetic and copies ran while one was open for 43% of the time, Pallas kernels for 0%

commit v1 on v0

--- a/solution.py
+++ b/solution.py
@@ -6,6 +6,16 @@
 
 TILE = 128
 NEG = -1e30
+
+
+def load_shifts_all(bus_axis, z):
+    r1 = jnp.concatenate(
+        lax.all_to_all(
+            jnp.stack(jnp.split(z, lax.axis_size(bus_axis), axis=1), axis=0), bus_axis, 0, 0
+        ),
+        0,
+    )
+    return r1
 
 
 def from_behind(value, axis, steps):
@@ -71,7 +81,7 @@
 def body(queries, key_proj, value_proj, out_grad, tile_order, doc_tiles):
     key_rows, value_rows = (
         lax.all_to_all(key_proj, "head", split_axis=1, concat_axis=0, tiled=True),
-        lax.all_to_all(value_proj, "head", split_axis=1, concat_axis=0, tiled=True),
+        load_shifts_all("head", value_proj),
     )
     row_count = queries.shape[0]
     kv_local = key_rows.shape[1]

time: 185 us -> 205 us (1.11)
  other arithmetic: 43.5 us -> 60.6 us
    le x15, other arithmetic: 9.68 us -> 15.1 us  [block_mask(): key_pos[None, :] <= query_pos[:, None]]
    mul x16, other arithmetic: 6.43 us -> 11.7 us  [row_info(): positions = (shard_tiles[:, None] * tile_len + offsets[None, :]).reshape(-1)]
    reduce_sum x16, other arithmetic: 7.69 us -> 12 us  [row_info(): jnp.sum((shard_tiles[:, None] >= doc_ends[None, :]).astype(jnp.int32), ax...]
    unnamed x39 -> x35, local copies, waits for them, and re-layouts: 10.8 us -> 9.38 us
  transfers between devices with their start and end apart: 50 -> 50, of which waited for: 27 -> 27; matrix products, arithmetic and copies ran while one was open for 43% -> 47% of each run, Pallas kernels for 0% -> 0%
where the time goes in v1:
time: 205 us; the launch traced here: 203 us
  other arithmetic  60.6 us (30%)
  waiting for transfers between devices  45.3 us (22%)
  matrix products  40.2 us (20%)
  starting transfers between devices  33.3 us (16%)
  local copies, waits for them, and re-layouts  20.8 us (10%)
    ppermute x46, waiting for transfers between devices, from_behind(): return lax.ppermute(value, axis, pairs)  35.8 us
    ppermute x46, starting transfers between devices, from_behind(): return lax.ppermute(value, axis, pairs)  18.3 us
    le x15, other arithmetic, block_mask(): key_pos[None, :] <= query_pos[:, None]  15.1 us
    dot_general x16, matrix products, block_scores(): jnp.einsum('tngd,knd->tngk', query_block, key_block, preferred_element_ty...  14.9 us
    reduce_sum x16, other arithmetic, row_info(): jnp.sum((shard_tiles[:, None] >= doc_ends[None, :]).astype(jnp.int32), ax...  12 us
    mul x16, other arithmetic, row_info(): positions = (shard_tiles[:, None] * tile_len + offsets[None, :]).reshape(-1)  11.7 us
    unnamed x35, local copies, waits for them, and re-layouts  9.38 us
    while x37, local copies, waits for them, and re-layouts  8.96 us
  transfers between devices with their start and end apart: 50, of which 27 were waited for; matrix products, arithmetic and copies ran while one was open for 47% of the time, Pallas kernels for 0%

profile of v1, /device:TPU:0, one launch (start us, length us, event | category | flops | bytes accessed | tf_op | source)
XLA Modules:
  0.0 202.9 jit_solution(906296815873927551)
XLA Ops:
  0.7 1.6 copy.91
  2.2 5.2 %all-to-all-start = ((bf16[64,4,128]{2,0,1:T(8,128)(2,1)}), bf16[64,4,128]{2,0,1:T(8,128)(2,1)S(1)}, u32[]{:S(2)}, u32[]{:S(2)}) async-start(bf16[64,4,128]{2,0,1:T(8,128)(2,1)} %copy.91), calls=%async_computation | async-start | bytes 131072 | tf_op jit(solution)/shard_map/all_to_all | solution.py:83
  7.4 1.1 fusion.69
  11.0 1.2 all-to-all-done
  12.2 3.3 %all-to-all-start.1 = ((bf16[4,64,1,128]{3,1,2,0:T(8,128)(2,1)}), bf16[4,64,1,128]{3,1,2,0:T(8,128)(2,1)S(1)}, u32[]{:S(2)}, u32[]{:S(2)}) async-start(bf16[4,64,1,128]{3,1,2,0:T(8,128)(2,1)} %pad_maximum_fusion), calls=%async_computation.1 | async-start | bytes 131072 | tf_op jit(solution)/shard_map/all_to_all | solution.py:13
  16.3 1.1 copy.139
  18.2 2.2 %all-to-all-done.1 = bf16[4,64,1,128]{3,1,2,0:T(8,128)(2,1)S(1)} async-done(((bf16[4,64,1,128]{3,1,2,0:T(8,128)(2,1)}), bf16[4,64,1,128]{3,1,2,0:T(8,128)(2,1)S(1)}, u32[]{:S(2)}, u32[]{:S(2)}) %all-to-all-start.1) | async-done | bytes 65568 | tf_op jit(solution)/shard_map/all_to_all | solution.py:13
  21.0 1.4 fusion.46
  22.4 1.3 fusion.50
  23.7 1.5 fusion.52
  25.3 1.5 copy.100
  26.8 62.3 %while.48 = (s32[]{:T(128)}, bf16[256,1,128]{2,0,1:T(8,128)(2,1)}, bf16[256,1,128]{2,0,1:T(8,128)(2,1)}, f32[256,1,8]{0,2,1:T(8,128)S(1)}, f32[256,1,8]{0,2,1:T(...) while((s32[]{:T(128)}, bf16[256,1,128]{2,0,1:T(8,128)(2,1)}, ...), condition=%wide.region_8.9_spmd.clone, body=%wide.region_4.0_spmd.clone.sunk | while | flops 274930240 | bytes 10232312 | solution.py:130
  26.9 1.7 collective-permute-start.1
  28.6 1.3 add_bitcast_fusion.9
  34.8 0.9 fusion.102
  35.8 1.4 collective-permute-start.1
  37.2 1.3 add_bitcast_fusion.9
  43.7 0.9 fusion.102
  44.7 1.2 collective-permute-start.1
  45.9 1.3 add_bitcast_fusion.9
  52.6 0.9 fusion.102
  53.7 1.3 add_bitcast_fusion.9
  57.5 1.9 collective-permute-done
  61.6 0.9 fusion.102
  62.6 1.3 add_bitcast_fusion.9
  66.4 1.9 collective-permute-done
  70.5 0.9 fusion.102
  71.5 1.3 add_bitcast_fusion.9
  75.3 1.9 collective-permute-done
  79.4 0.9 fusion.102
  80.4 1.3 add_bitcast_fusion.9
  84.2 1.9 collective-permute-done
  90.6 3.3 %multiply_reduce_fusion = (f32[256,8]{1,0:T(8,128)}, bf16[256,1,8,128]{3,2,0,1:T(8,128)(2,1)}) fusion(bf16[256,8,128]{2,1,0:T(8,128)(2,1)} %param.13, f32[256,8]{1,0:T(8,128)} %copy.101, f32[256,1,8,128]{3,0,2,1:T(8,128)S(1)} %get-tuple-element.648), kind=kLoop, calls=%fused_computation.83 | loop fusion | flops 1570816 | bytes 2113536 | tf_op jit(solution)/shard_map/reduce_sum | solution.py:134
  93.9 1.0 copy.104
  94.9 89.1 %while.49 = (s32[]{:T(128)}, bf16[256,1,128]{2,0,1:T(8,128)(2,1)S(1)}, bf16[256,1,128]{2,0,1:T(8,128)(2,1)S(1)}, f32[256,1,128]{2,0,1:T(8,128)S(1)}, f32[256,1,1...) while((s32[]{:T(128)}, ...), condition=%wide.region_12.13_spmd.clone, body=%wide.region_10.12_spmd.clone.sunk | while | flops 675742272 | bytes 16081516 | solution.py:156
  97.6 1.3 bitcast_select_fusion.4
  100.3 1.4 collective-permute-start.5
  102.6 2.7 %collective-permute-done.4 = bf16[256,1,128]{2,0,1:T(8,128)(2,1)S(1)} collective-permute-done((bf16[256,1,128]{2,0,1:T(8,128)(2,1)S(1)}, bf16[256,1,128]{2,0,1:T(8,128)(2,1)S(1)}, u32[]{:S(2)}, u32[]{:S(2)}) %collective-permute-start.4) | collective-permute-done | bytes 65568 | tf_op jit(solution)/shard_map/while/body/eval_jaxpr/ppermute | solution.py:24
  108.7 1.3 bitcast_select_fusion.4
  111.4 1.5 collective-permute-start.5
  113.8 2.7 %collective-permute-done.4 = bf16[256,1,128]{2,0,1:T(8,128)(2,1)S(1)} collective-permute-done((bf16[256,1,128]{2,0,1:T(8,128)(2,1)S(1)}, bf16[256,1,128]{2,0,1:T(8,128)(2,1)S(1)}, u32[]{:S(2)}, u32[]{:S(2)}) %collective-permute-start.4) | collective-permute-done | bytes 65568 | tf_op jit(solution)/shard_map/while/body/eval_jaxpr/ppermute | solution.py:24
  119.9 1.3 bitcast_select_fusion.4
  122.5 1.5 collective-permute-start.5
  124.9 2.6 %collective-permute-done.4 = bf16[256,1,128]{2,0,1:T(8,128)(2,1)S(1)} collective-permute-done((bf16[256,1,128]{2,0,1:T(8,128)(2,1)S(1)}, bf16[256,1,128]{2,0,1:T(8,128)(2,1)S(1)}, u32[]{:S(2)}, u32[]{:S(2)}) %collective-permute-start.4) | collective-permute-done | bytes 65568 | tf_op jit(solution)/shard_map/while/body/eval_jaxpr/ppermute | solution.py:24
  131.0 1.3 bitcast_select_fusion.4
  133.7 1.5 collective-permute-start.5
  136.1 2.6 %collective-permute-done.4 = bf16[256,1,128]{2,0,1:T(8,128)(2,1)S(1)} collective-permute-done((bf16[256,1,128]{2,0,1:T(8,128)(2,1)S(1)}, bf16[256,1,128]{2,0,1:T(8,128)(2,1)S(1)}, u32[]{:S(2)}, u32[]{:S(2)}) %collective-permute-start.4) | collective-permute-done | bytes 65568 | tf_op jit(solution)/shard_map/while/body/eval_jaxpr/ppermute | solution.py:24
  142.1 1.3 bitcast_select_fusion.4
  144.8 1.5 collective-permute-start.5
  147.2 2.6 %collective-permute-done.4 = bf16[256,1,128]{2,0,1:T(8,128)(2,1)S(1)} collective-permute-done((bf16[256,1,128]{2,0,1:T(8,128)(2,1)S(1)}, bf16[256,1,128]{2,0,1:T(8,128)(2,1)S(1)}, u32[]{:S(2)}, u32[]{:S(2)}) %collective-permute-start.4) | collective-permute-done | bytes 65568 | tf_op jit(solution)/shard_map/while/body/eval_jaxpr/ppermute | solution.py:24
  153.3 1.3 bitcast_select_fusion.4
  156.0 1.5 collective-permute-start.5
  158.4 2.6 %collective-permute-done.4 = bf16[256,1,128]{2,0,1:T(8,128)(2,1)S(1)} collective-permute-done((bf16[256,1,128]{2,0,1:T(8,128)(2,1)S(1)}, bf16[256,1,128]{2,0,1:T(8,128)(2,1)S(1)}, u32[]{:S(2)}, u32[]{:S(2)}) %collective-permute-start.4) | collective-permute-done | bytes 65568 | tf_op jit(solution)/shard_map/while/body/eval_jaxpr/ppermute | solution.py:24
  164.4 1.3 bitcast_select_fusion.4
  167.1 1.5 collective-permute-start.5
  169.5 2.6 %collective-permute-done.4 = bf16[256,1,128]{2,0,1:T(8,128)(2,1)S(1)} collective-permute-done((bf16[256,1,128]{2,0,1:T(8,128)(2,1)S(1)}, bf16[256,1,128]{2,0,1:T(8,128)(2,1)S(1)}, u32[]{:S(2)}, u32[]{:S(2)}) %collective-permute-start.4) | collective-permute-done | bytes 65568 | tf_op jit(solution)/shard_map/while/body/eval_jaxpr/ppermute | solution.py:24
  175.6 1.3 bitcast_select_fusion.4
  178.3 1.5 collective-permute-start.5
  180.7 2.6 %collective-permute-done.4 = bf16[256,1,128]{2,0,1:T(8,128)(2,1)S(1)} collective-permute-done((bf16[256,1,128]{2,0,1:T(8,128)(2,1)S(1)}, bf16[256,1,128]{2,0,1:T(8,128)(2,1)S(1)}, u32[]{:S(2)}, u32[]{:S(2)}) %collective-permute-start.4) | collective-permute-done | bytes 65568 | tf_op jit(solution)/shard_map/while/body/eval_jaxpr/ppermute | solution.py:24
  185.9 3.3 %all-to-all-start.2 = ((bf16[4,2,4096]{2,1,0:T(2,128)(2,1)}), bf16[4,2,4096]{2,1,0:T(2,128)(2,1)S(1)}, u32[]{:S(2)}, u32[]{:S(2)}) async-start(bf16[4,2,4096]{2,1,0:T(2,128)(2,1)} %reshape.650), calls=%async_computation.2 | async-start | bytes 131072 | tf_op jit(solution)/shard_map/all_to_all | solution.py:169
  190.5 3.5 %all-to-all-done.2 = bf16[4,2,4096]{2,1,0:T(2,128)(2,1)S(1)} async-done(((bf16[4,2,4096]{2,1,0:T(2,128)(2,1)}), bf16[4,2,4096]{2,1,0:T(2,128)(2,1)S(1)}, u32[]{:S(2)}, u32[]{:S(2)}) %all-to-all-start.2) | async-done | bytes 65568 | tf_op jit(solution)/shard_map/all_to_all | solution.py:169
  194.0 3.3 %all-to-all-start.3 = ((bf16[4,2,4096]{2,1,0:T(2,128)(2,1)}), bf16[4,2,4096]{2,1,0:T(2,128)(2,1)S(1)}, u32[]{:S(2)}, u32[]{:S(2)}) async-start(bf16[4,2,4096]{2,1,0:T(2,128)(2,1)} %reshape.652), calls=%async_computation.3 | async-start | bytes 131072 | tf_op jit(solution)/shard_map/all_to_all | solution.py:170
  197.3 1.5 fusion.61
  199.5 2.6 %all-to-all-done.3 = bf16[4,2,4096]{2,1,0:T(2,128)(2,1)S(1)} async-done(((bf16[4,2,4096]{2,1,0:T(2,128)(2,1)}), bf16[4,2,4096]{2,1,0:T(2,128)(2,1)S(1)}, u32[]{:S(2)}, u32[]{:S(2)}) %all-to-all-start.3) | async-done | bytes 65568 | tf_op jit(solution)/shard_map/all_to_all | solution.py:170
  (302 shorter events, 90.7 us)
Async XLA Ops:
  0.6 20.4 %copy-start.4 = (bf16[256,8,128]{2,1,0:T(8,128)(2,1)S(1)}, bf16[256,8,128]{2,1,0:T(8,128)(2,1)}, u32[]{:S(2)}) copy-start(bf16[256,8,128]{2,1,0:T(8,128)(2,1)} %param.10) | copy-start | bytes 1572868
  0.6 16.8 %copy-start.5 = (bf16[256,8,128]{2,1,0:T(8,128)(2,1)S(1)}, bf16[256,8,128]{2,1,0:T(8,128)(2,1)}, u32[]{:S(2)}) copy-start(bf16[256,8,128]{2,1,0:T(8,128)(2,1)} %param.13) | copy-start | bytes 1572868
  2.2 10.0 %all-to-all-start = ((bf16[64,4,128]{2,0,1:T(8,128)(2,1)}), bf16[64,4,128]{2,0,1:T(8,128)(2,1)S(1)}, u32[]{:S(2)}, u32[]{:S(2)}) async-start(bf16[64,4,128]{2,0,1:T(8,128)(2,1)} %copy.91), calls=%async_computation | async-start | bytes 131072 | tf_op jit(solution)/shard_map/all_to_all | solution.py:83
  9.3 7.0 %copy-start.9 = (s32[4,1]{0,1:T(1,128)}, s32[4,1]{0,1:T(1,128)S(1)}, u32[]{:S(2)}) copy-start(s32[4,1]{0,1:T(1,128)S(1)} %reduce-window.8) | copy-start | bytes 52
  10.1 6.2 %copy-start.7 = (s32[2]{0:T(128)}, s32[2]{0:T(128)S(1)}, u32[]{:S(2)}) copy-start(s32[2]{0:T(128)S(1)} %get-tuple-element.1241) | copy-start | bytes 28
  10.3 6.0 %copy-start.8 = (s32[2]{0:T(128)}, s32[2]{0:T(128)S(1)}, u32[]{:S(2)}) copy-start(s32[2]{0:T(128)S(1)} %fusion.64) | copy-start | bytes 28
  12.2 10.2 %copy-start = (bf16[64,4,128]{2,0,1:T(8,128)(2,1)}, bf16[64,4,128]{2,0,1:T(8,128)(2,1)S(1)}, u32[]{:S(2)}) copy-start(bf16[64,4,128]{2,0,1:T(8,128)(2,1)S(1)} %all-to-all-done) | copy-start | bytes 196612
  12.2 8.1 %all-to-all-start.1 = ((bf16[4,64,1,128]{3,1,2,0:T(8,128)(2,1)}), bf16[4,64,1,128]{3,1,2,0:T(8,128)(2,1)S(1)}, u32[]{:S(2)}, u32[]{:S(2)}) async-start(bf16[4,64,1,128]{3,1,2,0:T(8,128)(2,1)} %pad_maximum_fusion), calls=%async_computation.1 | async-start | bytes 131072 | tf_op jit(solution)/shard_map/all_to_all | solution.py:13
  20.3 3.4 %copy-start.2 = (bf16[4,64,1,128]{3,1,2,0:T(8,128)(2,1)}, bf16[4,64,1,128]{3,1,2,0:T(8,128)(2,1)S(1)}, u32[]{:S(2)}) copy-start(bf16[4,64,1,128]{3,1,2,0:T(8,128)(2,1)S(1)} %all-to-all-done.1) | copy-start | bytes 196612
  21.0 2.7 %copy-start.6 = (pred[256,256]{0,1:T(8,128)(4,1)S(1)}, pred[256,256]{0,1:T(8,128)(4,1)}, u32[]{:S(2)}) copy-start(pred[256,256]{0,1:T(8,128)(4,1)} %compare_and_fusion.2) | copy-start | bytes 196612
  26.9 5.8 %collective-permute-start = (bf16[256,1,128]{2,0,1:T(8,128)(2,1)}, bf16[256,1,128]{2,0,1:T(8,128)(2,1)S(1)}, u32[]{:S(2)}, u32[]{:S(2)}) collective-permute-start(bf16[256,1,128]{2,0,1:T(8,128)(2,1)} %get-tuple-element.1192), channel_id=1, source_target_pairs={{0,4},{4,8},{8,12},{12,16},{16,20},{20,24},{24,28},{28,0},{1,5},{5... | collective-permute-start | bytes 196616 | tf_op jit(solution)/shard_map/while/body/eval_jaxpr/ppermute | solution.py:24
  26.9 7.3 %collective-permute-start.1 = (bf16[256,1,128]{2,0,1:T(8,128)(2,1)}, bf16[256,1,128]{2,0,1:T(8,128)(2,1)S(1)}, u32[]{:S(2)}, u32[]{:S(2)}) collective-permute-start(bf16[256,1,128]{2,0,1:T(8,128)(2,1)} %get-tuple-element.1193), channel_id=1, source_target_pairs={{0,4},{4,8},{8,12},{12,16},{16,20},{20,24},{24,28},{28,0},{1,5},{5... | collective-permute-start | bytes 196616 | tf_op jit(solution)/shard_map/while/body/eval_jaxpr/ppermute | solution.py:24
  35.8 5.8 %collective-permute-start = (bf16[256,1,128]{2,0,1:T(8,128)(2,1)}, bf16[256,1,128]{2,0,1:T(8,128)(2,1)S(1)}, u32[]{:S(2)}, u32[]{:S(2)}) collective-permute-start(bf16[256,1,128]{2,0,1:T(8,128)(2,1)} %get-tuple-element.1192), channel_id=1, source_target_pairs={{0,4},{4,8},{8,12},{12,16},{16,20},{20,24},{24,28},{28,0},{1,5},{5... | collective-permute-start | bytes 196616 | tf_op jit(solution)/shard_map/while/body/eval_jaxpr/ppermute | solution.py:24
  35.8 7.3 %collective-permute-start.1 = (bf16[256,1,128]{2,0,1:T(8,128)(2,1)}, bf16[256,1,128]{2,0,1:T(8,128)(2,1)S(1)}, u32[]{:S(2)}, u32[]{:S(2)}) collective-permute-start(bf16[256,1,128]{2,0,1:T(8,128)(2,1)} %get-tuple-element.1193), channel_id=1, source_target_pairs={{0,4},{4,8},{8,12},{12,16},{16,20},{20,24},{24,28},{28,0},{1,5},{5... | collective-permute-start | bytes 196616 | tf_op jit(solution)/shard_map/while/body/eval_jaxpr/ppermute | solution.py:24
  44.7 5.8 %collective-permute-start = (bf16[256,1,128]{2,0,1:T(8,128)(2,1)}, bf16[256,1,128]{2,0,1:T(8,128)(2,1)S(1)}, u32[]{:S(2)}, u32[]{:S(2)}) collective-permute-start(bf16[256,1,128]{2,0,1:T(8,128)(2,1)} %get-tuple-element.1192), channel_id=1, source_target_pairs={{0,4},{4,8},{8,12},{12,16},{16,20},{20,24},{24,28},{28,0},{1,5},{5... | collective-permute-start | bytes 196616 | tf_op jit(solution)/shard_map/while/body/eval_jaxpr/ppermute | solution.py:24
  44.7 7.3 %collective-permute-start.1 = (bf16[256,1,128]{2,0,1:T(8,128)(2,1)}, bf16[256,1,128]{2,0,1:T(8,128)(2,1)S(1)}, u32[]{:S(2)}, u32[]{:S(2)}) collective-permute-start(bf16[256,1,128]{2,0,1:T(8,128)(2,1)} %get-tuple-element.1193), channel_id=1, source_target_pairs={{0,4},{4,8},{8,12},{12,16},{16,20},{20,24},{24,28},{28,0},{1,5},{5... | collective-permute-start | bytes 196616 | tf_op jit(solution)/shard_map/while/body/eval_jaxpr/ppermute | solution.py:24
  53.6 5.8 %collective-permute-start = (bf16[256,1,128]{2,0,1:T(8,128)(2,1)}, bf16[256,1,128]{2,0,1:T(8,128)(2,1)S(1)}, u32[]{:S(2)}, u32[]{:S(2)}) collective-permute-start(bf16[256,1,128]{2,0,1:T(8,128)(2,1)} %get-tuple-element.1192), channel_id=1, source_target_pairs={{0,4},{4,8},{8,12},{12,16},{16,20},{20,24},{24,28},{28,0},{1,5},{5... | collective-permute-start | bytes 196616 | tf_op jit(solution)/shard_map/while/body/eval_jaxpr/ppermute | solution.py:24
  53.6 7.3 %collective-permute-start.1 = (bf16[256,1,128]{2,0,1:T(8,128)(2,1)}, bf16[256,1,128]{2,0,1:T(8,128)(2,1)S(1)}, u32[]{:S(2)}, u32[]{:S(2)}) collective-permute-start(bf16[256,1,128]{2,0,1:T(8,128)(2,1)} %get-tuple-element.1193), channel_id=1, source_target_pairs={{0,4},{4,8},{8,12},{12,16},{16,20},{20,24},{24,28},{28,0},{1,5},{5... | collective-permute-start | bytes 196616 | tf_op jit(solution)/shard_map/while/body/eval_jaxpr/ppermute | solution.py:24
  62.5 5.8 %collective-permute-start = (bf16[256,1,128]{2,0,1:T(8,128)(2,1)}, bf16[256,1,128]{2,0,1:T(8,128)(2,1)S(1)}, u32[]{:S(2)}, u32[]{:S(2)}) collective-permute-start(bf16[256,1,128]{2,0,1:T(8,128)(2,1)} %get-tuple-element.1192), channel_id=1, source_target_pairs={{0,4},{4,8},{8,12},{12,16},{16,20},{20,24},{24,28},{28,0},{1,5},{5... | collective-permute-start | bytes 196616 | tf_op jit(solution)/shard_map/while/body/eval_jaxpr/ppermute | solution.py:24
  62.5 7.3 %collective-permute-start.1 = (bf16[256,1,128]{2,0,1:T(8,128)(2,1)}, bf16[256,1,128]{2,0,1:T(8,128)(2,1)S(1)}, u32[]{:S(2)}, u32[]{:S(2)}) collective-permute-start(bf16[256,1,128]{2,0,1:T(8,128)(2,1)} %get-tuple-element.1193), channel_id=1, source_target_pairs={{0,4},{4,8},{8,12},{12,16},{16,20},{20,24},{24,28},{28,0},{1,5},{5... | collective-permute-start | bytes 196616 | tf_op jit(solution)/shard_map/while/body/eval_jaxpr/ppermute | solution.py:24
  71.4 5.8 %collective-permute-start = (bf16[256,1,128]{2,0,1:T(8,128)(2,1)}, bf16[256,1,128]{2,0,1:T(8,128)(2,1)S(1)}, u32[]{:S(2)}, u32[]{:S(2)}) collective-permute-start(bf16[256,1,128]{2,0,1:T(8,128)(2,1)} %get-tuple-element.1192), channel_id=1, source_target_pairs={{0,4},{4,8},{8,12},{12,16},{16,20},{20,24},{24,28},{28,0},{1,5},{5... | collective-permute-start | bytes 196616 | tf_op jit(solution)/shard_map/while/body/eval_jaxpr/ppermute | solution.py:24
  71.5 7.3 %collective-permute-start.1 = (bf16[256,1,128]{2,0,1:T(8,128)(2,1)}, bf16[256,1,128]{2,0,1:T(8,128)(2,1)S(1)}, u32[]{:S(2)}, u32[]{:S(2)}) collective-permute-start(bf16[256,1,128]{2,0,1:T(8,128)(2,1)} %get-tuple-element.1193), channel_id=1, source_target_pairs={{0,4},{4,8},{8,12},{12,16},{16,20},{20,24},{24,28},{28,0},{1,5},{5... | collective-permute-start | bytes 196616 | tf_op jit(solution)/shard_map/while/body/eval_jaxpr/ppermute | solution.py:24
  80.3 5.8 %collective-permute-start = (bf16[256,1,128]{2,0,1:T(8,128)(2,1)}, bf16[256,1,128]{2,0,1:T(8,128)(2,1)S(1)}, u32[]{:S(2)}, u32[]{:S(2)}) collective-permute-start(bf16[256,1,128]{2,0,1:T(8,128)(2,1)} %get-tuple-element.1192), channel_id=1, source_target_pairs={{0,4},{4,8},{8,12},{12,16},{16,20},{20,24},{24,28},{28,0},{1,5},{5... | collective-permute-start | bytes 196616 | tf_op jit(solution)/shard_map/while/body/eval_jaxpr/ppermute | solution.py:24
  80.4 7.3 %collective-permute-start.1 = (bf16[256,1,128]{2,0,1:T(8,128)(2,1)}, bf16[256,1,128]{2,0,1:T(8,128)(2,1)S(1)}, u32[]{:S(2)}, u32[]{:S(2)}) collective-permute-start(bf16[256,1,128]{2,0,1:T(8,128)(2,1)} %get-tuple-element.1193), channel_id=1, source_target_pairs={{0,4},{4,8},{8,12},{12,16},{16,20},{20,24},{24,28},{28,0},{1,5},{5... | collective-permute-start | bytes 196616 | tf_op jit(solution)/shard_map/while/body/eval_jaxpr/ppermute | solution.py:24
  89.2 5.7 %copy-start.1 = (bf16[64,4,128]{2,0,1:T(8,128)(2,1)S(1)}, bf16[64,4,128]{2,0,1:T(8,128)(2,1)}, u32[]{:S(2)}) copy-start(bf16[64,4,128]{2,0,1:T(8,128)(2,1)} %copy-done) | copy-start | bytes 196612
  89.2 5.7 %copy-start.3 = (bf16[4,64,1,128]{3,1,2,0:T(8,128)(2,1)S(1)}, bf16[4,64,1,128]{3,1,2,0:T(8,128)(2,1)}, u32[]{:S(2)}) copy-start(bf16[4,64,1,128]{3,1,2,0:T(8,128)(2,1)} %copy-done.2) | copy-start | bytes 196612
  94.9 11.1 %collective-permute-start.2 = (bf16[256,1,128]{2,0,1:T(8,128)(2,1)S(1)}, bf16[256,1,128]{2,0,1:T(8,128)(2,1)S(1)}, u32[]{:S(2)}, u32[]{:S(2)}) collective-permute-start(bf16[256,1,128]{2,0,1:T(8,128)(2,1)S(1)} %copy.167), channel_id=1, source_target_pairs={{0,4},{4,8},{8,12},{12,16},{16,20},{20,24},{24,28},{28,0},{1,5},{5... | collective-permute-start | bytes 196616 | tf_op jit(solution)/shard_map/while/body/eval_jaxpr/ppermute | solution.py:24
  95.0 11.0 %collective-permute-start.3 = (bf16[256,1,128]{2,0,1:T(8,128)(2,1)S(1)}, bf16[256,1,128]{2,0,1:T(8,128)(2,1)S(1)}, u32[]{:S(2)}, u32[]{:S(2)}) collective-permute-start(bf16[256,1,128]{2,0,1:T(8,128)(2,1)S(1)} %copy.168), channel_id=1, source_target_pairs={{0,4},{4,8},{8,12},{12,16},{16,20},{20,24},{24,28},{28,0},{1,5},{5... | collective-permute-start | bytes 196616 | tf_op jit(solution)/shard_map/while/body/eval_jaxpr/ppermute | solution.py:24
  99.7 5.5 %collective-permute-start.4 = (bf16[256,1,128]{2,0,1:T(8,128)(2,1)S(1)}, bf16[256,1,128]{2,0,1:T(8,128)(2,1)S(1)}, u32[]{:S(2)}, u32[]{:S(2)}) collective-permute-start(bf16[256,1,128]{2,0,1:T(8,128)(2,1)S(1)} %fusion.115), channel_id=1, source_target_pairs={{0,4},{4,8},{8,12},{12,16},{16,20},{20,24},{24,28},{28,0},{1,5},{5... | collective-permute-start | bytes 196616 | tf_op jit(solution)/shard_map/while/body/eval_jaxpr/ppermute | solution.py:24
  100.3 5.7 %collective-permute-start.5 = (bf16[256,1,128]{2,0,1:T(8,128)(2,1)S(1)}, bf16[256,1,128]{2,0,1:T(8,128)(2,1)S(1)}, u32[]{:S(2)}, u32[]{:S(2)}) collective-permute-start(bf16[256,1,128]{2,0,1:T(8,128)(2,1)S(1)} %fusion.116), channel_id=1, source_target_pairs={{0,4},{4,8},{8,12},{12,16},{16,20},{20,24},{24,28},{28,0},{1,5},{5... | collective-permute-start | bytes 196616 | tf_op jit(solution)/shard_map/while/body/eval_jaxpr/ppermute | solution.py:24
  106.1 11.1 %collective-permute-start.2 = (bf16[256,1,128]{2,0,1:T(8,128)(2,1)S(1)}, bf16[256,1,128]{2,0,1:T(8,128)(2,1)S(1)}, u32[]{:S(2)}, u32[]{:S(2)}) collective-permute-start(bf16[256,1,128]{2,0,1:T(8,128)(2,1)S(1)} %copy.167), channel_id=1, source_target_pairs={{0,4},{4,8},{8,12},{12,16},{16,20},{20,24},{24,28},{28,0},{1,5},{5... | collective-permute-start | bytes 196616 | tf_op jit(solution)/shard_map/while/body/eval_jaxpr/ppermute | solution.py:24
  106.1 11.0 %collective-permute-start.3 = (bf16[256,1,128]{2,0,1:T(8,128)(2,1)S(1)}, bf16[256,1,128]{2,0,1:T(8,128)(2,1)S(1)}, u32[]{:S(2)}, u32[]{:S(2)}) collective-permute-start(bf16[256,1,128]{2,0,1:T(8,128)(2,1)S(1)} %copy.168), channel_id=1, source_target_pairs={{0,4},{4,8},{8,12},{12,16},{16,20},{20,24},{24,28},{28,0},{1,5},{5... | collective-permute-start | bytes 196616 | tf_op jit(solution)/shard_map/while/body/eval_jaxpr/ppermute | solution.py:24
  110.9 5.5 %collective-permute-start.4 = (bf16[256,1,128]{2,0,1:T(8,128)(2,1)S(1)}, bf16[256,1,128]{2,0,1:T(8,128)(2,1)S(1)}, u32[]{:S(2)}, u32[]{:S(2)}) collective-permute-start(bf16[256,1,128]{2,0,1:T(8,128)(2,1)S(1)} %fusion.115), channel_id=1, source_target_pairs={{0,4},{4,8},{8,12},{12,16},{16,20},{20,24},{24,28},{28,0},{1,5},{5... | collective-permute-start | bytes 196616 | tf_op jit(solution)/shard_map/while/body/eval_jaxpr/ppermute | solution.py:24
  111.4 5.7 %collective-permute-start.5 = (bf16[256,1,128]{2,0,1:T(8,128)(2,1)S(1)}, bf16[256,1,128]{2,0,1:T(8,128)(2,1)S(1)}, u32[]{:S(2)}, u32[]{:S(2)}) collective-permute-start(bf16[256,1,128]{2,0,1:T(8,128)(2,1)S(1)} %fusion.116), channel_id=1, source_target_pairs={{0,4},{4,8},{8,12},{12,16},{16,20},{20,24},{24,28},{28,0},{1,5},{5... | collective-permute-start | bytes 196616 | tf_op jit(solution)/shard_map/while/body/eval_jaxpr/ppermute | solution.py:24
  117.2 11.1 %collective-permute-start.2 = (bf16[256,1,128]{2,0,1:T(8,128)(2,1)S(1)}, bf16[256,1,128]{2,0,1:T(8,128)(2,1)S(1)}, u32[]{:S(2)}, u32[]{:S(2)}) collective-permute-start(bf16[256,1,128]{2,0,1:T(8,128)(2,1)S(1)} %copy.167), channel_id=1, source_target_pairs={{0,4},{4,8},{8,12},{12,16},{16,20},{20,24},{24,28},{28,0},{1,5},{5... | collective-permute-start | bytes 196616 | tf_op jit(solution)/shard_map/while/body/eval_jaxpr/ppermute | solution.py:24
  117.3 11.0 %collective-permute-start.3 = (bf16[256,1,128]{2,0,1:T(8,128)(2,1)S(1)}, bf16[256,1,128]{2,0,1:T(8,128)(2,1)S(1)}, u32[]{:S(2)}, u32[]{:S(2)}) collective-permute-start(bf16[256,1,128]{2,0,1:T(8,128)(2,1)S(1)} %copy.168), channel_id=1, source_target_pairs={{0,4},{4,8},{8,12},{12,16},{16,20},{20,24},{24,28},{28,0},{1,5},{5... | collective-permute-start | bytes 196616 | tf_op jit(solution)/shard_map/while/body/eval_jaxpr/ppermute | solution.py:24
  122.0 5.5 %collective-permute-start.4 = (bf16[256,1,128]{2,0,1:T(8,128)(2,1)S(1)}, bf16[256,1,128]{2,0,1:T(8,128)(2,1)S(1)}, u32[]{:S(2)}, u32[]{:S(2)}) collective-permute-start(bf16[256,1,128]{2,0,1:T(8,128)(2,1)S(1)} %fusion.115), channel_id=1, source_target_pairs={{0,4},{4,8},{8,12},{12,16},{16,20},{20,24},{24,28},{28,0},{1,5},{5... | collective-permute-start | bytes 196616 | tf_op jit(solution)/shard_map/while/body/eval_jaxpr/ppermute | solution.py:24
  122.5 5.7 %collective-permute-start.5 = (bf16[256,1,128]{2,0,1:T(8,128)(2,1)S(1)}, bf16[256,1,128]{2,0,1:T(8,128)(2,1)S(1)}, u32[]{:S(2)}, u32[]{:S(2)}) collective-permute-start(bf16[256,1,128]{2,0,1:T(8,128)(2,1)S(1)} %fusion.116), channel_id=1, source_target_pairs={{0,4},{4,8},{8,12},{12,16},{16,20},{20,24},{24,28},{28,0},{1,5},{5... | collective-permute-start | bytes 196616 | tf_op jit(solution)/shard_map/while/body/eval_jaxpr/ppermute | solution.py:24
  128.3 11.1 %collective-permute-start.2 = (bf16[256,1,128]{2,0,1:T(8,128)(2,1)S(1)}, bf16[256,1,128]{2,0,1:T(8,128)(2,1)S(1)}, u32[]{:S(2)}, u32[]{:S(2)}) collective-permute-start(bf16[256,1,128]{2,0,1:T(8,128)(2,1)S(1)} %copy.167), channel_id=1, source_target_pairs={{0,4},{4,8},{8,12},{12,16},{16,20},{20,24},{24,28},{28,0},{1,5},{5... | collective-permute-start | bytes 196616 | tf_op jit(solution)/shard_map/while/body/eval_jaxpr/ppermute | solution.py:24
  128.4 11.0 %collective-permute-start.3 = (bf16[256,1,128]{2,0,1:T(8,128)(2,1)S(1)}, bf16[256,1,128]{2,0,1:T(8,128)(2,1)S(1)}, u32[]{:S(2)}, u32[]{:S(2)}) collective-permute-start(bf16[256,1,128]{2,0,1:T(8,128)(2,1)S(1)} %copy.168), channel_id=1, source_target_pairs={{0,4},{4,8},{8,12},{12,16},{16,20},{20,24},{24,28},{28,0},{1,5},{5... | collective-permute-start | bytes 196616 | tf_op jit(solution)/shard_map/while/body/eval_jaxpr/ppermute | solution.py:24
  133.2 5.5 %collective-permute-start.4 = (bf16[256,1,128]{2,0,1:T(8,128)(2,1)S(1)}, bf16[256,1,128]{2,0,1:T(8,128)(2,1)S(1)}, u32[]{:S(2)}, u32[]{:S(2)}) collective-permute-start(bf16[256,1,128]{2,0,1:T(8,128)(2,1)S(1)} %fusion.115), channel_id=1, source_target_pairs={{0,4},{4,8},{8,12},{12,16},{16,20},{20,24},{24,28},{28,0},{1,5},{5... | collective-permute-start | bytes 196616 | tf_op jit(solution)/shard_map/while/body/eval_jaxpr/ppermute | solution.py:24
  133.7 5.7 %collective-permute-start.5 = (bf16[256,1,128]{2,0,1:T(8,128)(2,1)S(1)}, bf16[256,1,128]{2,0,1:T(8,128)(2,1)S(1)}, u32[]{:S(2)}, u32[]{:S(2)}) collective-permute-start(bf16[256,1,128]{2,0,1:T(8,128)(2,1)S(1)} %fusion.116), channel_id=1, source_target_pairs={{0,4},{4,8},{8,12},{12,16},{16,20},{20,24},{24,28},{28,0},{1,5},{5... | collective-permute-start | bytes 196616 | tf_op jit(solution)/shard_map/while/body/eval_jaxpr/ppermute | solution.py:24
  139.5 11.1 %collective-permute-start.2 = (bf16[256,1,128]{2,0,1:T(8,128)(2,1)S(1)}, bf16[256,1,128]{2,0,1:T(8,128)(2,1)S(1)}, u32[]{:S(2)}, u32[]{:S(2)}) collective-permute-start(bf16[256,1,128]{2,0,1:T(8,128)(2,1)S(1)} %copy.167), channel_id=1, source_target_pairs={{0,4},{4,8},{8,12},{12,16},{16,20},{20,24},{24,28},{28,0},{1,5},{5... | collective-permute-start | bytes 196616 | tf_op jit(solution)/shard_map/while/body/eval_jaxpr/ppermute | solution.py:24
  139.6 11.0 %collective-permute-start.3 = (bf16[256,1,128]{2,0,1:T(8,128)(2,1)S(1)}, bf16[256,1,128]{2,0,1:T(8,128)(2,1)S(1)}, u32[]{:S(2)}, u32[]{:S(2)}) collective-permute-start(bf16[256,1,128]{2,0,1:T(8,128)(2,1)S(1)} %copy.168), channel_id=1, source_target_pairs={{0,4},{4,8},{8,12},{12,16},{16,20},{20,24},{24,28},{28,0},{1,5},{5... | collective-permute-start | bytes 196616 | tf_op jit(solution)/shard_map/while/body/eval_jaxpr/ppermute | solution.py:24
  144.3 5.5 %collective-permute-start.4 = (bf16[256,1,128]{2,0,1:T(8,128)(2,1)S(1)}, bf16[256,1,128]{2,0,1:T(8,128)(2,1)S(1)}, u32[]{:S(2)}, u32[]{:S(2)}) collective-permute-start(bf16[256,1,128]{2,0,1:T(8,128)(2,1)S(1)} %fusion.115), channel_id=1, source_target_pairs={{0,4},{4,8},{8,12},{12,16},{16,20},{20,24},{24,28},{28,0},{1,5},{5... | collective-permute-start | bytes 196616 | tf_op jit(solution)/shard_map/while/body/eval_jaxpr/ppermute | solution.py:24
  144.8 5.7 %collective-permute-start.5 = (bf16[256,1,128]{2,0,1:T(8,128)(2,1)S(1)}, bf16[256,1,128]{2,0,1:T(8,128)(2,1)S(1)}, u32[]{:S(2)}, u32[]{:S(2)}) collective-permute-start(bf16[256,1,128]{2,0,1:T(8,128)(2,1)S(1)} %fusion.116), channel_id=1, source_target_pairs={{0,4},{4,8},{8,12},{12,16},{16,20},{20,24},{24,28},{28,0},{1,5},{5... | collective-permute-start | bytes 196616 | tf_op jit(solution)/shard_map/while/body/eval_jaxpr/ppermute | solution.py:24
  150.6 11.1 %collective-permute-start.2 = (bf16[256,1,128]{2,0,1:T(8,128)(2,1)S(1)}, bf16[256,1,128]{2,0,1:T(8,128)(2,1)S(1)}, u32[]{:S(2)}, u32[]{:S(2)}) collective-permute-start(bf16[256,1,128]{2,0,1:T(8,128)(2,1)S(1)} %copy.167), channel_id=1, source_target_pairs={{0,4},{4,8},{8,12},{12,16},{16,20},{20,24},{24,28},{28,0},{1,5},{5... | collective-permute-start | bytes 196616 | tf_op jit(solution)/shard_map/while/body/eval_jaxpr/ppermute | solution.py:24
  150.7 11.0 %collective-permute-start.3 = (bf16[256,1,128]{2,0,1:T(8,128)(2,1)S(1)}, bf16[256,1,128]{2,0,1:T(8,128)(2,1)S(1)}, u32[]{:S(2)}, u32[]{:S(2)}) collective-permute-start(bf16[256,1,128]{2,0,1:T(8,128)(2,1)S(1)} %copy.168), channel_id=1, source_target_pairs={{0,4},{4,8},{8,12},{12,16},{16,20},{20,24},{24,28},{28,0},{1,5},{5... | collective-permute-start | bytes 196616 | tf_op jit(solution)/shard_map/while/body/eval_jaxpr/ppermute | solution.py:24
  155.5 5.5 %collective-permute-start.4 = (bf16[256,1,128]{2,0,1:T(8,128)(2,1)S(1)}, bf16[256,1,128]{2,0,1:T(8,128)(2,1)S(1)}, u32[]{:S(2)}, u32[]{:S(2)}) collective-permute-start(bf16[256,1,128]{2,0,1:T(8,128)(2,1)S(1)} %fusion.115), channel_id=1, source_target_pairs={{0,4},{4,8},{8,12},{12,16},{16,20},{20,24},{24,28},{28,0},{1,5},{5... | collective-permute-start | bytes 196616 | tf_op jit(solution)/shard_map/while/body/eval_jaxpr/ppermute | solution.py:24
  156.0 5.7 %collective-permute-start.5 = (bf16[256,1,128]{2,0,1:T(8,128)(2,1)S(1)}, bf16[256,1,128]{2,0,1:T(8,128)(2,1)S(1)}, u32[]{:S(2)}, u32[]{:S(2)}) collective-permute-start(bf16[256,1,128]{2,0,1:T(8,128)(2,1)S(1)} %fusion.116), channel_id=1, source_target_pairs={{0,4},{4,8},{8,12},{12,16},{16,20},{20,24},{24,28},{28,0},{1,5},{5... | collective-permute-start | bytes 196616 | tf_op jit(solution)/shard_map/while/body/eval_jaxpr/ppermute | solution.py:24
  161.8 11.1 %collective-permute-start.2 = (bf16[256,1,128]{2,0,1:T(8,128)(2,1)S(1)}, bf16[256,1,128]{2,0,1:T(8,128)(2,1)S(1)}, u32[]{:S(2)}, u32[]{:S(2)}) collective-permute-start(bf16[256,1,128]{2,0,1:T(8,128)(2,1)S(1)} %copy.167), channel_id=1, source_target_pairs={{0,4},{4,8},{8,12},{12,16},{16,20},{20,24},{24,28},{28,0},{1,5},{5... | collective-permute-start | bytes 196616 | tf_op jit(solution)/shard_map/while/body/eval_jaxpr/ppermute | solution.py:24
  161.9 11.0 %collective-permute-start.3 = (bf16[256,1,128]{2,0,1:T(8,128)(2,1)S(1)}, bf16[256,1,128]{2,0,1:T(8,128)(2,1)S(1)}, u32[]{:S(2)}, u32[]{:S(2)}) collective-permute-start(bf16[256,1,128]{2,0,1:T(8,128)(2,1)S(1)} %copy.168), channel_id=1, source_target_pairs={{0,4},{4,8},{8,12},{12,16},{16,20},{20,24},{24,28},{28,0},{1,5},{5... | collective-permute-start | bytes 196616 | tf_op jit(solution)/shard_map/while/body/eval_jaxpr/ppermute | solution.py:24
  166.6 5.5 %collective-permute-start.4 = (bf16[256,1,128]{2,0,1:T(8,128)(2,1)S(1)}, bf16[256,1,128]{2,0,1:T(8,128)(2,1)S(1)}, u32[]{:S(2)}, u32[]{:S(2)}) collective-permute-start(bf16[256,1,128]{2,0,1:T(8,128)(2,1)S(1)} %fusion.115), channel_id=1, source_target_pairs={{0,4},{4,8},{8,12},{12,16},{16,20},{20,24},{24,28},{28,0},{1,5},{5... | collective-permute-start | bytes 196616 | tf_op jit(solution)/shard_map/while/body/eval_jaxpr/ppermute | solution.py:24
  167.1 5.7 %collective-permute-start.5 = (bf16[256,1,128]{2,0,1:T(8,128)(2,1)S(1)}, bf16[256,1,128]{2,0,1:T(8,128)(2,1)S(1)}, u32[]{:S(2)}, u32[]{:S(2)}) collective-permute-start(bf16[256,1,128]{2,0,1:T(8,128)(2,1)S(1)} %fusion.116), channel_id=1, source_target_pairs={{0,4},{4,8},{8,12},{12,16},{16,20},{20,24},{24,28},{28,0},{1,5},{5... | collective-permute-start | bytes 196616 | tf_op jit(solution)/shard_map/while/body/eval_jaxpr/ppermute | solution.py:24
  172.9 11.1 %collective-permute-start.2 = (bf16[256,1,128]{2,0,1:T(8,128)(2,1)S(1)}, bf16[256,1,128]{2,0,1:T(8,128)(2,1)S(1)}, u32[]{:S(2)}, u32[]{:S(2)}) collective-permute-start(bf16[256,1,128]{2,0,1:T(8,128)(2,1)S(1)} %copy.167), channel_id=1, source_target_pairs={{0,4},{4,8},{8,12},{12,16},{16,20},{20,24},{24,28},{28,0},{1,5},{5... | collective-permute-start | bytes 196616 | tf_op jit(solution)/shard_map/while/body/eval_jaxpr/ppermute | solution.py:24
  173.0 11.0 %collective-permute-start.3 = (bf16[256,1,128]{2,0,1:T(8,128)(2,1)S(1)}, bf16[256,1,128]{2,0,1:T(8,128)(2,1)S(1)}, u32[]{:S(2)}, u32[]{:S(2)}) collective-permute-start(bf16[256,1,128]{2,0,1:T(8,128)(2,1)S(1)} %copy.168), channel_id=1, source_target_pairs={{0,4},{4,8},{8,12},{12,16},{16,20},{20,24},{24,28},{28,0},{1,5},{5... | collective-permute-start | bytes 196616 | tf_op jit(solution)/shard_map/while/body/eval_jaxpr/ppermute | solution.py:24
  177.7 5.5 %collective-permute-start.4 = (bf16[256,1,128]{2,0,1:T(8,128)(2,1)S(1)}, bf16[256,1,128]{2,0,1:T(8,128)(2,1)S(1)}, u32[]{:S(2)}, u32[]{:S(2)}) collective-permute-start(bf16[256,1,128]{2,0,1:T(8,128)(2,1)S(1)} %fusion.115), channel_id=1, source_target_pairs={{0,4},{4,8},{8,12},{12,16},{16,20},{20,24},{24,28},{28,0},{1,5},{5... | collective-permute-start | bytes 196616 | tf_op jit(solution)/shard_map/while/body/eval_jaxpr/ppermute | solution.py:24
  178.3 5.7 %collective-permute-start.5 = (bf16[256,1,128]{2,0,1:T(8,128)(2,1)S(1)}, bf16[256,1,128]{2,0,1:T(8,128)(2,1)S(1)}, u32[]{:S(2)}, u32[]{:S(2)}) collective-permute-start(bf16[256,1,128]{2,0,1:T(8,128)(2,1)S(1)} %fusion.116), channel_id=1, source_target_pairs={{0,4},{4,8},{8,12},{12,16},{16,20},{20,24},{24,28},{28,0},{1,5},{5... | collective-permute-start | bytes 196616 | tf_op jit(solution)/shard_map/while/body/eval_jaxpr/ppermute | solution.py:24
  185.9 8.1 %all-to-all-start.2 = ((bf16[4,2,4096]{2,1,0:T(2,128)(2,1)}), bf16[4,2,4096]{2,1,0:T(2,128)(2,1)S(1)}, u32[]{:S(2)}, u32[]{:S(2)}) async-start(bf16[4,2,4096]{2,1,0:T(2,128)(2,1)} %reshape.650), calls=%async_computation.2 | async-start | bytes 131072 | tf_op jit(solution)/shard_map/all_to_all | solution.py:169
  194.0 8.1 %all-to-all-start.3 = ((bf16[4,2,4096]{2,1,0:T(2,128)(2,1)}), bf16[4,2,4096]{2,1,0:T(2,128)(2,1)S(1)}, u32[]{:S(2)}, u32[]{:S(2)}) async-start(bf16[4,2,4096]{2,1,0:T(2,128)(2,1)} %reshape.652), calls=%async_computation.3 | async-start | bytes 131072 | tf_op jit(solution)/shard_map/all_to_all | solution.py:170
